TPU v7x, 32 devices: a whole 2x2x4 slice. The times are simulated.
32 devices in a mesh: dp: 4 (over z), section: 4 (over y, x), mp: 2 (over core).
Axes of the slice: x: 2, y: 2, z: 4, core: 2. Of those that a mesh axis runs over, the one named last changes fastest.
Arguments:
- inputs: bfloat16 [4, 128, 3072], P(None, 'dp'), may hold values from -6 to 6
- target: bfloat16 [4, 128, 3072], P(None, 'dp', 'mp'), may hold values from -6 to 6
- gains: float32 [4, 3072], P('section'), may hold values from 0.5 to 1.5
- weights: bfloat16 [4, 3072, 3072], P('section', 'dp', 'mp'), may hold values from -0.109375 to 0.109375
- probes: float32 [4, 4, 3072], P(None, 'section', 'dp'), may hold values from -6 to 6
Outputs:
- hvp: float32 [4, 4, 3072], P(None, 'section', 'dp')
- probes_next: float32 [4, 4, 3072], P(None, 'section', 'dp')
All inputs are finite; a program needn't handle non-finite values.
Results may differ from a plain program's by a relative error of at most 0.013.
Values may be sent and summed in bfloat16 or wider, within the bound.
A program may use at most 128 MiB of HBM per device.

v0:
```python
import math

import jax
import jax.numpy as jnp
from jax import lax
from jax.sharding import PartitionSpec as P

EPS = 1e-05
ETA = 0.5


def from_behind(value, axis, steps):
    count = lax.axis_size(axis)
    initial, last = (max(0, -steps), min(count, count - steps))
    return lax.ppermute(value, axis, [(source, source + steps) for source in range(initial, last)])


def norm_parts(whole_input):
    values = whole_input.astype(jnp.float32)
    hidden = values[0]
    tangent = values[1:]
    scale_inv = lax.rsqrt(jnp.mean(hidden * hidden, axis=-1, keepdims=True) + EPS)
    normed = hidden * scale_inv
    scale_dot = -(scale_inv**3) * jnp.mean(hidden * tangent, axis=-1, keepdims=True)
    normed_dot = tangent * scale_inv + hidden * scale_dot
    return (hidden, tangent, scale_inv, normed, scale_dot, normed_dot)


def section_forward(whole_input, own_cols, gain_row, probe_dirs, weight):
    hidden, tangent, scale_inv, normed, scale_dot, normed_dot = norm_parts(whole_input)
    mixed_in = normed * gain_row
    mixed_dot = normed_dot * gain_row + normed[None] * probe_dirs[:, None, :]
    operand = jnp.concatenate([mixed_in[None], mixed_dot], axis=0).astype(jnp.bfloat16)
    flattened = operand.reshape(-1, operand.shape[-1])
    product = jnp.dot(flattened, weight, preferred_element_type=jnp.float32)
    product = product.reshape(operand.shape[:2] + (weight.shape[1],))
    active = jnp.tanh(product[0])
    active_dot = (1.0 - active * active) * product[1:]
    section_activity = jnp.concatenate([active[None], active_dot], axis=0)
    residual = own_cols.astype(jnp.float32)
    return ((residual + section_activity).astype(jnp.bfloat16), section_activity)


def pre_stack(section_activity, cotangent):
    incoming = cotangent.astype(jnp.float32)
    active = section_activity[0]
    active_dot = section_activity[1:]
    derivative = 1.0 - active * active
    pre_grad = incoming[0] * derivative
    pre_dot = incoming[1:] * derivative - 2.0 * active * active_dot * incoming[0]
    return jnp.concatenate([pre_grad[None], pre_dot], axis=0).astype(jnp.bfloat16)


def section_backward(whole_input, gain_row, probe_dirs, weight, section_activity, cotangent):
    hidden, tangent, scale_inv, normed, scale_dot, normed_dot = norm_parts(whole_input)
    operand = pre_stack(section_activity, cotangent)
    flattened = operand.reshape(-1, operand.shape[-1])
    returned = jnp.dot(flattened, weight.T, preferred_element_type=jnp.float32)
    returned = returned.reshape(operand.shape[:2] + (weight.shape[0],))
    mixed_grad = returned[0]
    mixed_dot = returned[1:]
    gain_dot = jnp.sum(mixed_dot * normed + mixed_grad * normed_dot, axis=1)
    normed_grad = mixed_grad * gain_row
    normed_gdot = mixed_dot * gain_row + mixed_grad * probe_dirs[:, None, :]
    features = hidden.shape[-1]
    inner_grad = jnp.sum(normed_grad * hidden, axis=-1, keepdims=True)
    inner_dot = jnp.sum(normed_gdot * hidden + normed_grad * tangent, axis=-1, keepdims=True)
    cube_scale = scale_inv**3 / features
    grad_in = scale_inv * normed_grad - cube_scale * hidden * inner_grad
    grad_dot = (
        scale_dot * normed_grad
        + scale_inv * normed_gdot
        - 3.0 * scale_inv * scale_inv * scale_dot / features * hidden * inner_grad
        - cube_scale * tangent * inner_grad
        - cube_scale * hidden * inner_dot
    )
    return (jnp.concatenate([grad_in[None], grad_dot], axis=0), gain_dot)


def local(inputs, target, gains, weights, probes):
    sections = lax.axis_size("section")
    section_pos = lax.axis_index("section")
    core_pos = lax.axis_index("mp")
    batches, micro_batch_tokens, features = inputs.shape
    directions = probes.shape[0]
    column_block = weights.shape[2]
    stacked_rows = directions + 1
    weight = lax.all_gather(weights, "dp", axis=1, tiled=True)[0]
    probe_dirs = lax.all_gather(probes.astype(jnp.bfloat16), "dp", axis=2, tiled=True).astype(
        probes.dtype
    )[:, 0, :]
    gain_row = gains[0]
    offset_own = core_pos * column_block
    ticks = batches + sections - 1
    blank = jnp.zeros((directions, micro_batch_tokens, features), jnp.bfloat16)
    whole_stash = jnp.zeros((batches, stacked_rows, micro_batch_tokens, features), jnp.bfloat16)
    active_stash = jnp.zeros((batches, stacked_rows, micro_batch_tokens, column_block), jnp.float32)
    output_stash = jnp.zeros(
        (batches, stacked_rows, micro_batch_tokens, column_block), jnp.bfloat16
    )
    arriving_input = jnp.zeros((stacked_rows, micro_batch_tokens, features), jnp.bfloat16)

    def forward_tick(moment, carry):
        arriving_input, whole_stash, active_stash, output_stash = carry
        batch_id = moment - section_pos
        valid = (batch_id >= 0) & (batch_id < batches)
        buffer_slot_index = jnp.clip(batch_id, 0, batches - 1)
        first = jnp.concatenate(
            [lax.dynamic_index_in_dim(inputs, buffer_slot_index, 0, keepdims=True), blank], axis=0
        )
        received = arriving_input
        whole_input = jnp.where(section_pos == 0, first, received)
        own_cols = lax.dynamic_slice_in_dim(whole_input, offset_own, column_block, 2)

        def apply_section(saved_buffers):
            section_result, section_activity = section_forward(
                whole_input, own_cols, gain_row, probe_dirs, weight
            )
            saved_whole_rows = lax.dynamic_update_index_in_dim(
                saved_buffers[0], whole_input, buffer_slot_index, 0
            )
            saved_active_rows = lax.dynamic_update_index_in_dim(
                saved_buffers[1], section_activity, buffer_slot_index, 0
            )
            saved_output_rows = lax.dynamic_update_index_in_dim(
                saved_buffers[2], section_result, buffer_slot_index, 0
            )
            return ((saved_whole_rows, saved_active_rows, saved_output_rows), section_result)

        def bypass_section(saved_buffers):
            return (
                saved_buffers,
                jnp.zeros((stacked_rows, micro_batch_tokens, column_block), jnp.bfloat16),
            )

        saved_buffers, section_result = lax.cond(
            valid, apply_section, bypass_section, (whole_stash, active_stash, output_stash)
        )
        joined = lax.all_gather(section_result, "mp", axis=2, tiled=True)
        arriving_input = from_behind(joined, "section", 1)
        return (arriving_input,) + saved_buffers

    carried = lax.fori_loop(
        0, ticks, forward_tick, (arriving_input, whole_stash, active_stash, output_stash)
    )
    whole_stash, active_stash, output_stash = (carried[1], carried[2], carried[3])

    def backward_tick(moment, carry):
        incoming, accumulated = carry
        batch_id = moment - (sections - 1 - section_pos)
        valid = (batch_id >= 0) & (batch_id < batches)
        buffer_slot_index = jnp.clip(batch_id, 0, batches - 1)
        finished = lax.dynamic_index_in_dim(output_stash, buffer_slot_index, 0, keepdims=False)
        aimed = lax.dynamic_index_in_dim(target, buffer_slot_index, 0, keepdims=False)
        error = (finished[0].astype(jnp.float32) - aimed.astype(jnp.float32)).astype(jnp.bfloat16)
        last_cotangent = jnp.concatenate([error[None], finished[1:]], axis=0)
        cotangent = jnp.where(section_pos == sections - 1, last_cotangent, incoming)
        whole_input = lax.dynamic_index_in_dim(whole_stash, buffer_slot_index, 0, keepdims=False)
        section_activity = lax.dynamic_index_in_dim(
            active_stash, buffer_slot_index, 0, keepdims=False
        )

        def run_back(running):
            grads, gain_dot = section_backward(
                whole_input, gain_row, probe_dirs, weight, section_activity, cotangent
            )
            return (running + gain_dot, grads)

        def skip_back(running):
            return (running, jnp.zeros((stacked_rows, micro_batch_tokens, features), jnp.float32))

        accumulated, grads = lax.cond(valid, run_back, skip_back, accumulated)
        summed = lax.psum_scatter(
            grads.astype(jnp.bfloat16), "mp", scatter_dimension=2, tiled=True
        ).astype(jnp.float32)
        passed = (summed + cotangent.astype(jnp.float32)).astype(jnp.bfloat16)
        incoming = from_behind(passed, "section", -1)
        return (incoming, accumulated)

    start_cot = jnp.zeros((stacked_rows, micro_batch_tokens, column_block), jnp.bfloat16)
    start_acc = jnp.zeros((directions, features), jnp.float32)
    finished_cot, accumulated = lax.fori_loop(0, ticks, backward_tick, (start_cot, start_acc))
    divisor = batches * micro_batch_tokens * lax.axis_size("dp")
    own_probe = probes[:, 0, :]
    owned = lax.psum_scatter(
        accumulated.astype(jnp.bfloat16), "dp", scatter_dimension=1, tiled=True
    ).astype(jnp.float32)
    owned = lax.psum(owned, "mp")
    curvature = owned / divisor
    moved = own_probe + ETA * curvature
    local_gram = jnp.dot(moved, moved.T, precision=lax.Precision.HIGHEST)
    gram = lax.psum(local_gram, ("dp", "section"))
    factor = jnp.linalg.cholesky(gram)
    rotated = jax.scipy.linalg.solve_triangular(factor, moved, lower=True) * math.sqrt(
        sections * features
    )
    return (curvature[:, None, :], rotated[:, None, :])


def solution(mesh):
    in_specs = (
        P(None, "dp", None),
        P(None, "dp", "mp"),
        P("section", None),
        P("section", "dp", "mp"),
        P(None, "section", "dp"),
    )
    out_specs = (P(None, "section", "dp"), P(None, "section", "dp"))
    return jax.shard_map(local, mesh=mesh, in_specs=in_specs, out_specs=out_specs, check_vma=False)
```

profile of v0, /device:TPU:0, one launch (start us, length us, event | category | flops | bytes accessed | tf_op | source)
XLA Modules:
  0.0 834.7 jit_solution(14646740566021370455)
XLA Ops:
  7.9 14.8 %all_gather.15 = bf16[4,1,3072]{2,0,1:T(4,128)(2,1)S(1)} all-gather(bf16[4,1,768]{2,0,1:T(4,128)(2,1)S(1)} %copy.26), channel_id=1, replica_groups=mesh['dp'=4,'section'=4,'mp'=2] {'dp'}, dimensions={2}, use_global_device_ids=true | all-gather | bytes 30720 | tf_op jit(solution)/shard_map/all_gather | solution.py:89
  22.8 156.3 %all-gather.2.cloned.1.call-done = bf16[1,3072,1536]{2,1,0:T(8,128)(2,1)} async-done(((bf16[1,768,1536]{2,1,0:T(8,128)(2,1)}), bf16[1,3072,1536]{2,1,0:T(8,128)(2,1)}) %all-gather.2.cloned.1.call-update) | async-done | bytes 9437200 | tf_op jit(solution)/shard_map/all_gather | solution.py:88
  185.5 253.7 %while.41 = (s32[]{:T(128)}, bf16[5,32,3072]{2,1,0:T(8,128)(2,1)S(1)}, bf16[4,5,32,3072]{3,2,1,0:T(8,128)(2,1)}, f32[4,5,32,1536]{3,2,1,0:T(8,128)}, bf16[4,5,32...) while((s32[]{:T(128)}, ...), condition=%wide.region_5.6_spmd, body=%wide.region_0.5_spmd.sunk | while | flops 1516978304 | bytes 78327592 | solution.py:143
  199.0 21.5 %collective-permute-done = bf16[5,32,3072]{2,1,0:T(8,128)(2,1)S(1)} collective-permute-done((bf16[5,32,3072]{2,1,0:T(8,128)(2,1)S(1)}, bf16[5,32,3072]{2,1,0:T(8,128)(2,1)S(1)}, u32[]{:S(2)}, u32[]{:S(2)}) %collective-permute-start) | collective-permute-done | bytes 983072 | tf_op jit(solution)/shard_map/while/body/eval_jaxpr/ppermute | solution.py:15
  237.1 21.2 %collective-permute-done = bf16[5,32,3072]{2,1,0:T(8,128)(2,1)S(1)} collective-permute-done((bf16[5,32,3072]{2,1,0:T(8,128)(2,1)S(1)}, bf16[5,32,3072]{2,1,0:T(8,128)(2,1)S(1)}, u32[]{:S(2)}, u32[]{:S(2)}) %collective-permute-start) | collective-permute-done | bytes 983072 | tf_op jit(solution)/shard_map/while/body/eval_jaxpr/ppermute | solution.py:15
  274.9 21.2 %collective-permute-done = bf16[5,32,3072]{2,1,0:T(8,128)(2,1)S(1)} collective-permute-done((bf16[5,32,3072]{2,1,0:T(8,128)(2,1)S(1)}, bf16[5,32,3072]{2,1,0:T(8,128)(2,1)S(1)}, u32[]{:S(2)}, u32[]{:S(2)}) %collective-permute-start) | collective-permute-done | bytes 983072 | tf_op jit(solution)/shard_map/while/body/eval_jaxpr/ppermute | solution.py:15
  312.7 21.2 %collective-permute-done = bf16[5,32,3072]{2,1,0:T(8,128)(2,1)S(1)} collective-permute-done((bf16[5,32,3072]{2,1,0:T(8,128)(2,1)S(1)}, bf16[5,32,3072]{2,1,0:T(8,128)(2,1)S(1)}, u32[]{:S(2)}, u32[]{:S(2)}) %collective-permute-start) | collective-permute-done | bytes 983072 | tf_op jit(solution)/shard_map/while/body/eval_jaxpr/ppermute | solution.py:15
  336.5 14.0 %collective-permute-start = (bf16[5,32,3072]{2,1,0:T(8,128)(2,1)S(1)}, bf16[5,32,3072]{2,1,0:T(8,128)(2,1)S(1)}, u32[]{:S(2)}, u32[]{:S(2)}) collective-permute-start(bf16[5,32,3072]{2,1,0:T(8,128)(2,1)S(1)} %all_gather.18), channel_id=1, source_target_pairs={{0,2},{2,4},{4,6},{1,3},{3,5},{5,7},{8,10},{10,12},{12,14},{9,11},... | collective-permute-start | bytes 2949128 | tf_op jit(solution)/shard_map/while/body/eval_jaxpr/ppermute | solution.py:15
  350.5 21.2 %collective-permute-done = bf16[5,32,3072]{2,1,0:T(8,128)(2,1)S(1)} collective-permute-done((bf16[5,32,3072]{2,1,0:T(8,128)(2,1)S(1)}, bf16[5,32,3072]{2,1,0:T(8,128)(2,1)S(1)}, u32[]{:S(2)}, u32[]{:S(2)}) %collective-permute-start) | collective-permute-done | bytes 983072 | tf_op jit(solution)/shard_map/while/body/eval_jaxpr/ppermute | solution.py:15
  379.2 21.2 %collective-permute-done = bf16[5,32,3072]{2,1,0:T(8,128)(2,1)S(1)} collective-permute-done((bf16[5,32,3072]{2,1,0:T(8,128)(2,1)S(1)}, bf16[5,32,3072]{2,1,0:T(8,128)(2,1)S(1)}, u32[]{:S(2)}, u32[]{:S(2)}) %collective-permute-start) | collective-permute-done | bytes 983072 | tf_op jit(solution)/shard_map/while/body/eval_jaxpr/ppermute | solution.py:15
  403.0 14.9 %collective-permute-start = (bf16[5,32,3072]{2,1,0:T(8,128)(2,1)S(1)}, bf16[5,32,3072]{2,1,0:T(8,128)(2,1)S(1)}, u32[]{:S(2)}, u32[]{:S(2)}) collective-permute-start(bf16[5,32,3072]{2,1,0:T(8,128)(2,1)S(1)} %all_gather.18), channel_id=1, source_target_pairs={{0,2},{2,4},{4,6},{1,3},{3,5},{5,7},{8,10},{10,12},{12,14},{9,11},... | collective-permute-start | bytes 2949128 | tf_op jit(solution)/shard_map/while/body/eval_jaxpr/ppermute | solution.py:15
  418.0 21.2 %collective-permute-done = bf16[5,32,3072]{2,1,0:T(8,128)(2,1)S(1)} collective-permute-done((bf16[5,32,3072]{2,1,0:T(8,128)(2,1)S(1)}, bf16[5,32,3072]{2,1,0:T(8,128)(2,1)S(1)}, u32[]{:S(2)}, u32[]{:S(2)}) %collective-permute-start) | collective-permute-done | bytes 983072 | tf_op jit(solution)/shard_map/while/body/eval_jaxpr/ppermute | solution.py:15
  439.3 313.1 %while.42 = (s32[]{:T(128)}, bf16[5,32,1536]{2,1,0:T(8,128)(2,1)S(1)}, f32[4,3072]{1,0:T(4,128)S(1)}, s32[]{:T(128)}, pred[]{:T(512)}, /*index=5*/bf16[4,5,32,15...) while((s32[]{:T(128)}, ...), condition=%wide.region_15.16_spmd, body=%wide.region_6.15_spmd.sunk | while | flops 1527402112 | bytes 61585872 | solution.py:182
  442.5 31.9 %reduce-scatter.7.cloned.1.call-done = bf16[5,32,1536]{2,1,0:T(8,128)(2,1)} async-done(((bf16[5,32,3072]{2,1,0:T(8,128)(2,1)}), bf16[5,32,1536]{2,1,0:T(8,128)(2,1)}) %reduce-scatter.7.cloned.1.call-update) | async-done | bytes 491536 | tf_op jit(solution)/shard_map/while/body/eval_jaxpr/reduce_scatter | solution.py:173
  476.9 14.0 %collective-permute-done.1 = bf16[5,32,1536]{2,1,0:T(8,128)(2,1)S(1)} collective-permute-done((bf16[5,32,1536]{2,1,0:T(8,128)(2,1)S(1)}, bf16[5,32,1536]{2,1,0:T(8,128)(2,1)S(1)}, u32[]{:S(2)}, u32[]{:S(2)}) %collective-permute-start.1) | collective-permute-done | bytes 491552 | tf_op jit(solution)/shard_map/while/body/eval_jaxpr/ppermute | solution.py:15
  494.1 23.5 %reduce-scatter.7.cloned.1.call-done = bf16[5,32,1536]{2,1,0:T(8,128)(2,1)} async-done(((bf16[5,32,3072]{2,1,0:T(8,128)(2,1)}), bf16[5,32,1536]{2,1,0:T(8,128)(2,1)}) %reduce-scatter.7.cloned.1.call-update) | async-done | bytes 491536 | tf_op jit(solution)/shard_map/while/body/eval_jaxpr/reduce_scatter | solution.py:173
  520.0 14.0 %collective-permute-done.1 = bf16[5,32,1536]{2,1,0:T(8,128)(2,1)S(1)} collective-permute-done((bf16[5,32,1536]{2,1,0:T(8,128)(2,1)S(1)}, bf16[5,32,1536]{2,1,0:T(8,128)(2,1)S(1)}, u32[]{:S(2)}, u32[]{:S(2)}) %collective-permute-start.1) | collective-permute-done | bytes 491552 | tf_op jit(solution)/shard_map/while/body/eval_jaxpr/ppermute | solution.py:15
  537.2 24.4 %reduce-scatter.7.cloned.1.call-done = bf16[5,32,1536]{2,1,0:T(8,128)(2,1)} async-done(((bf16[5,32,3072]{2,1,0:T(8,128)(2,1)}), bf16[5,32,1536]{2,1,0:T(8,128)(2,1)}) %reduce-scatter.7.cloned.1.call-update) | async-done | bytes 491536 | tf_op jit(solution)/shard_map/while/body/eval_jaxpr/reduce_scatter | solution.py:173
  564.1 14.0 %collective-permute-done.1 = bf16[5,32,1536]{2,1,0:T(8,128)(2,1)S(1)} collective-permute-done((bf16[5,32,1536]{2,1,0:T(8,128)(2,1)S(1)}, bf16[5,32,1536]{2,1,0:T(8,128)(2,1)S(1)}, u32[]{:S(2)}, u32[]{:S(2)}) %collective-permute-start.1) | collective-permute-done | bytes 491552 | tf_op jit(solution)/shard_map/while/body/eval_jaxpr/ppermute | solution.py:15
  580.1 14.7 %conditional.5 = (f32[4,3072]{1,0:T(4,128)S(1)}, bf16[5,32,3072]{2,1,0:T(8,128)(2,1)S(1)}) conditional(s32[]{:T(128)} %convert_element_type.183, f32[4,3072]{1,0:T(4,128)S(1)} %get-tuple-element.1079, (bf16[5,32,1536]{2,1,0:T(8,128)(2,1)S(1)}, f32[4,5,32,1536]{3,2,1,0:T(8,128)}, s32[]{:T(128)}, bf16[3072,1536]{1,0:T(8,128)(2,1)}, ...), branch_computations={%region_7.7_spmd, %region_8.13_spmd} | conditional | flops 1525730944 | bytes 47233072 | solution.py:172
  595.8 9.8 %reduce-scatter.7.cloned.1.call-done = bf16[5,32,1536]{2,1,0:T(8,128)(2,1)} async-done(((bf16[5,32,3072]{2,1,0:T(8,128)(2,1)}), bf16[5,32,1536]{2,1,0:T(8,128)(2,1)}) %reduce-scatter.7.cloned.1.call-update) | async-done | bytes 491536 | tf_op jit(solution)/shard_map/while/body/eval_jaxpr/reduce_scatter | solution.py:173
  608.1 14.0 %collective-permute-done.1 = bf16[5,32,1536]{2,1,0:T(8,128)(2,1)S(1)} collective-permute-done((bf16[5,32,1536]{2,1,0:T(8,128)(2,1)S(1)}, bf16[5,32,1536]{2,1,0:T(8,128)(2,1)S(1)}, u32[]{:S(2)}, u32[]{:S(2)}) %collective-permute-start.1) | collective-permute-done | bytes 491552 | tf_op jit(solution)/shard_map/while/body/eval_jaxpr/ppermute | solution.py:15
  624.2 14.7 %conditional.5 = (f32[4,3072]{1,0:T(4,128)S(1)}, bf16[5,32,3072]{2,1,0:T(8,128)(2,1)S(1)}) conditional(s32[]{:T(128)} %convert_element_type.183, f32[4,3072]{1,0:T(4,128)S(1)} %get-tuple-element.1079, (bf16[5,32,1536]{2,1,0:T(8,128)(2,1)S(1)}, f32[4,5,32,1536]{3,2,1,0:T(8,128)}, s32[]{:T(128)}, bf16[3072,1536]{1,0:T(8,128)(2,1)}, ...), branch_computations={%region_7.7_spmd, %region_8.13_spmd} | conditional | flops 1525730944 | bytes 47233072 | solution.py:172
  639.8 9.8 %reduce-scatter.7.cloned.1.call-done = bf16[5,32,1536]{2,1,0:T(8,128)(2,1)} async-done(((bf16[5,32,3072]{2,1,0:T(8,128)(2,1)}), bf16[5,32,1536]{2,1,0:T(8,128)(2,1)}) %reduce-scatter.7.cloned.1.call-update) | async-done | bytes 491536 | tf_op jit(solution)/shard_map/while/body/eval_jaxpr/reduce_scatter | solution.py:173
  652.1 14.0 %collective-permute-done.1 = bf16[5,32,1536]{2,1,0:T(8,128)(2,1)S(1)} collective-permute-done((bf16[5,32,1536]{2,1,0:T(8,128)(2,1)S(1)}, bf16[5,32,1536]{2,1,0:T(8,128)(2,1)S(1)}, u32[]{:S(2)}, u32[]{:S(2)}) %collective-permute-start.1) | collective-permute-done | bytes 491552 | tf_op jit(solution)/shard_map/while/body/eval_jaxpr/ppermute | solution.py:15
  668.2 14.7 %conditional.5 = (f32[4,3072]{1,0:T(4,128)S(1)}, bf16[5,32,3072]{2,1,0:T(8,128)(2,1)S(1)}) conditional(s32[]{:T(128)} %convert_element_type.183, f32[4,3072]{1,0:T(4,128)S(1)} %get-tuple-element.1079, (bf16[5,32,1536]{2,1,0:T(8,128)(2,1)S(1)}, f32[4,5,32,1536]{3,2,1,0:T(8,128)}, s32[]{:T(128)}, bf16[3072,1536]{1,0:T(8,128)(2,1)}, ...), branch_computations={%region_7.7_spmd, %region_8.13_spmd} | conditional | flops 1525730944 | bytes 47233072 | solution.py:172
  683.9 9.8 %reduce-scatter.7.cloned.1.call-done = bf16[5,32,1536]{2,1,0:T(8,128)(2,1)} async-done(((bf16[5,32,3072]{2,1,0:T(8,128)(2,1)}), bf16[5,32,1536]{2,1,0:T(8,128)(2,1)}) %reduce-scatter.7.cloned.1.call-update) | async-done | bytes 491536 | tf_op jit(solution)/shard_map/while/body/eval_jaxpr/reduce_scatter | solution.py:173
  696.1 14.0 %collective-permute-done.1 = bf16[5,32,1536]{2,1,0:T(8,128)(2,1)S(1)} collective-permute-done((bf16[5,32,1536]{2,1,0:T(8,128)(2,1)S(1)}, bf16[5,32,1536]{2,1,0:T(8,128)(2,1)S(1)}, u32[]{:S(2)}, u32[]{:S(2)}) %collective-permute-start.1) | collective-permute-done | bytes 491552 | tf_op jit(solution)/shard_map/while/body/eval_jaxpr/ppermute | solution.py:15
  712.2 14.7 %conditional.5 = (f32[4,3072]{1,0:T(4,128)S(1)}, bf16[5,32,3072]{2,1,0:T(8,128)(2,1)S(1)}) conditional(s32[]{:T(128)} %convert_element_type.183, f32[4,3072]{1,0:T(4,128)S(1)} %get-tuple-element.1079, (bf16[5,32,1536]{2,1,0:T(8,128)(2,1)S(1)}, f32[4,5,32,1536]{3,2,1,0:T(8,128)}, s32[]{:T(128)}, bf16[3072,1536]{1,0:T(8,128)(2,1)}, ...), branch_computations={%region_7.7_spmd, %region_8.13_spmd} | conditional | flops 1525730944 | bytes 47233072 | solution.py:172
  738.3 14.0 %collective-permute-done.1 = bf16[5,32,1536]{2,1,0:T(8,128)(2,1)S(1)} collective-permute-done((bf16[5,32,1536]{2,1,0:T(8,128)(2,1)S(1)}, bf16[5,32,1536]{2,1,0:T(8,128)(2,1)S(1)}, u32[]{:S(2)}, u32[]{:S(2)}) %collective-permute-start.1) | collective-permute-done | bytes 491552 | tf_op jit(solution)/shard_map/while/body/eval_jaxpr/ppermute | solution.py:15
  753.6 26.4 %reduce-scatter.5.cloned.1.call-done = bf16[768,4]{1,0:T(8,128)(2,1)} async-done(((bf16[3072,4]{1,0:T(8,128)(2,1)}), bf16[768,4]{1,0:T(8,128)(2,1)}) %reduce-scatter.5.cloned.1.call-update) | async-done | bytes 6160
  784.5 40.0 %psum.15 = f32[4,4]{0,1:T(4,128)S(1)} all-reduce(f32[4,4]{0,1:T(4,128)S(1)} %fusion.25), channel_id=1, replica_groups=mesh['dp'=4,'section'=4,'mp'=2] {'dp','section'}, use_global_device_ids=true, to_apply=%region_18.19 | all-reduce | flops 16 | bytes 128 | tf_op jit(solution)/shard_map/psum | solution.py:192
  (276 shorter events, 235.8 us)
Async XLA Ops:
  7.2 171.9 %all-gather.2.cloned.1.call-start = ((), (), s32[]{:S(2)}) async-start(), calls=%async_computation.2 | async-start | bytes 11796480 | tf_op jit(solution)/shard_map/all_gather | solution.py:88
  183.9 1.6 copy-start.2
  186.5 3.7 copy-start
  197.7 22.9 %collective-permute-start = (bf16[5,32,3072]{2,1,0:T(8,128)(2,1)S(1)}, bf16[5,32,3072]{2,1,0:T(8,128)(2,1)S(1)}, u32[]{:S(2)}, u32[]{:S(2)}) collective-permute-start(bf16[5,32,3072]{2,1,0:T(8,128)(2,1)S(1)} %all_gather.18), channel_id=1, source_target_pairs={{0,2},{2,4},{4,6},{1,3},{3,5},{5,7},{8,10},{10,12},{12,14},{9,11},... | collective-permute-start | bytes 2949128 | tf_op jit(solution)/shard_map/while/body/eval_jaxpr/ppermute | solution.py:15
  221.5 3.7 copy-start
  232.6 25.7 %collective-permute-start = (bf16[5,32,3072]{2,1,0:T(8,128)(2,1)S(1)}, bf16[5,32,3072]{2,1,0:T(8,128)(2,1)S(1)}, u32[]{:S(2)}, u32[]{:S(2)}) collective-permute-start(bf16[5,32,3072]{2,1,0:T(8,128)(2,1)S(1)} %all_gather.18), channel_id=1, source_target_pairs={{0,2},{2,4},{4,6},{1,3},{3,5},{5,7},{8,10},{10,12},{12,14},{9,11},... | collective-permute-start | bytes 2949128 | tf_op jit(solution)/shard_map/while/body/eval_jaxpr/ppermute | solution.py:15
  259.3 3.7 copy-start
  270.4 25.7 %collective-permute-start = (bf16[5,32,3072]{2,1,0:T(8,128)(2,1)S(1)}, bf16[5,32,3072]{2,1,0:T(8,128)(2,1)S(1)}, u32[]{:S(2)}, u32[]{:S(2)}) collective-permute-start(bf16[5,32,3072]{2,1,0:T(8,128)(2,1)S(1)} %all_gather.18), channel_id=1, source_target_pairs={{0,2},{2,4},{4,6},{1,3},{3,5},{5,7},{8,10},{10,12},{12,14},{9,11},... | collective-permute-start | bytes 2949128 | tf_op jit(solution)/shard_map/while/body/eval_jaxpr/ppermute | solution.py:15
  297.1 3.7 copy-start
  308.3 25.6 %collective-permute-start = (bf16[5,32,3072]{2,1,0:T(8,128)(2,1)S(1)}, bf16[5,32,3072]{2,1,0:T(8,128)(2,1)S(1)}, u32[]{:S(2)}, u32[]{:S(2)}) collective-permute-start(bf16[5,32,3072]{2,1,0:T(8,128)(2,1)S(1)} %all_gather.18), channel_id=1, source_target_pairs={{0,2},{2,4},{4,6},{1,3},{3,5},{5,7},{8,10},{10,12},{12,14},{9,11},... | collective-permute-start | bytes 2949128 | tf_op jit(solution)/shard_map/while/body/eval_jaxpr/ppermute | solution.py:15
  336.5 35.3 %collective-permute-start = (bf16[5,32,3072]{2,1,0:T(8,128)(2,1)S(1)}, bf16[5,32,3072]{2,1,0:T(8,128)(2,1)S(1)}, u32[]{:S(2)}, u32[]{:S(2)}) collective-permute-start(bf16[5,32,3072]{2,1,0:T(8,128)(2,1)S(1)} %all_gather.18), channel_id=1, source_target_pairs={{0,2},{2,4},{4,6},{1,3},{3,5},{5,7},{8,10},{10,12},{12,14},{9,11},... | collective-permute-start | bytes 2949128 | tf_op jit(solution)/shard_map/while/body/eval_jaxpr/ppermute | solution.py:15
  374.3 26.1 %collective-permute-start = (bf16[5,32,3072]{2,1,0:T(8,128)(2,1)S(1)}, bf16[5,32,3072]{2,1,0:T(8,128)(2,1)S(1)}, u32[]{:S(2)}, u32[]{:S(2)}) collective-permute-start(bf16[5,32,3072]{2,1,0:T(8,128)(2,1)S(1)} %all_gather.18), channel_id=1, source_target_pairs={{0,2},{2,4},{4,6},{1,3},{3,5},{5,7},{8,10},{10,12},{12,14},{9,11},... | collective-permute-start | bytes 2949128 | tf_op jit(solution)/shard_map/while/body/eval_jaxpr/ppermute | solution.py:15
  403.0 36.2 %collective-permute-start = (bf16[5,32,3072]{2,1,0:T(8,128)(2,1)S(1)}, bf16[5,32,3072]{2,1,0:T(8,128)(2,1)S(1)}, u32[]{:S(2)}, u32[]{:S(2)}) collective-permute-start(bf16[5,32,3072]{2,1,0:T(8,128)(2,1)S(1)} %all_gather.18), channel_id=1, source_target_pairs={{0,2},{2,4},{4,6},{1,3},{3,5},{5,7},{8,10},{10,12},{12,14},{9,11},... | collective-permute-start | bytes 2949128 | tf_op jit(solution)/shard_map/while/body/eval_jaxpr/ppermute | solution.py:15
  439.3 35.2 %reduce-scatter.7.cloned.1.call-start = ((), (), s32[]{:S(2)}) async-start(), calls=%async_computation.4 | async-start | bytes 1474560 | tf_op jit(solution)/shard_map/while/body/eval_jaxpr/reduce_scatter | solution.py:173
  441.6 1.0 copy-start.1
  475.6 15.3 %collective-permute-start.1 = (bf16[5,32,1536]{2,1,0:T(8,128)(2,1)S(1)}, bf16[5,32,1536]{2,1,0:T(8,128)(2,1)S(1)}, u32[]{:S(2)}, u32[]{:S(2)}) collective-permute-start(bf16[5,32,1536]{2,1,0:T(8,128)(2,1)S(1)} %add_convert_fusion.5), channel_id=1, source_target_pairs={{2,0},{4,2},{6,4},{3,1},{5,3},{7,5},{10,8},{12,10},{14,12},{11,9},... | collective-permute-start | bytes 1474568 | tf_op jit(solution)/shard_map/while/body/eval_jaxpr/ppermute | solution.py:15
  490.9 26.7 %reduce-scatter.7.cloned.1.call-start = ((), (), s32[]{:S(2)}) async-start(), calls=%async_computation.4 | async-start | bytes 1474560 | tf_op jit(solution)/shard_map/while/body/eval_jaxpr/reduce_scatter | solution.py:173
  493.1 1.0 copy-start.1
  518.7 15.3 %collective-permute-start.1 = (bf16[5,32,1536]{2,1,0:T(8,128)(2,1)S(1)}, bf16[5,32,1536]{2,1,0:T(8,128)(2,1)S(1)}, u32[]{:S(2)}, u32[]{:S(2)}) collective-permute-start(bf16[5,32,1536]{2,1,0:T(8,128)(2,1)S(1)} %add_convert_fusion.5), channel_id=1, source_target_pairs={{2,0},{4,2},{6,4},{3,1},{5,3},{7,5},{10,8},{12,10},{14,12},{11,9},... | collective-permute-start | bytes 1474568 | tf_op jit(solution)/shard_map/while/body/eval_jaxpr/ppermute | solution.py:15
  534.0 27.6 %reduce-scatter.7.cloned.1.call-start = ((), (), s32[]{:S(2)}) async-start(), calls=%async_computation.4 | async-start | bytes 1474560 | tf_op jit(solution)/shard_map/while/body/eval_jaxpr/reduce_scatter | solution.py:173
  562.8 15.3 %collective-permute-start.1 = (bf16[5,32,1536]{2,1,0:T(8,128)(2,1)S(1)}, bf16[5,32,1536]{2,1,0:T(8,128)(2,1)S(1)}, u32[]{:S(2)}, u32[]{:S(2)}) collective-permute-start(bf16[5,32,1536]{2,1,0:T(8,128)(2,1)S(1)} %add_convert_fusion.5), channel_id=1, source_target_pairs={{2,0},{4,2},{6,4},{3,1},{5,3},{7,5},{10,8},{12,10},{14,12},{11,9},... | collective-permute-start | bytes 1474568 | tf_op jit(solution)/shard_map/while/body/eval_jaxpr/ppermute | solution.py:15
  578.1 27.6 %reduce-scatter.7.cloned.1.call-start = ((), (), s32[]{:S(2)}) async-start(), calls=%async_computation.4 | async-start | bytes 1474560 | tf_op jit(solution)/shard_map/while/body/eval_jaxpr/reduce_scatter | solution.py:173
  594.8 1.0 copy-start.1
  606.8 15.3 %collective-permute-start.1 = (bf16[5,32,1536]{2,1,0:T(8,128)(2,1)S(1)}, bf16[5,32,1536]{2,1,0:T(8,128)(2,1)S(1)}, u32[]{:S(2)}, u32[]{:S(2)}) collective-permute-start(bf16[5,32,1536]{2,1,0:T(8,128)(2,1)S(1)} %add_convert_fusion.5), channel_id=1, source_target_pairs={{2,0},{4,2},{6,4},{3,1},{5,3},{7,5},{10,8},{12,10},{14,12},{11,9},... | collective-permute-start | bytes 1474568 | tf_op jit(solution)/shard_map/while/body/eval_jaxpr/ppermute | solution.py:15
  622.1 27.6 %reduce-scatter.7.cloned.1.call-start = ((), (), s32[]{:S(2)}) async-start(), calls=%async_computation.4 | async-start | bytes 1474560 | tf_op jit(solution)/shard_map/while/body/eval_jaxpr/reduce_scatter | solution.py:173
  638.9 1.0 copy-start.1
  650.8 15.3 %collective-permute-start.1 = (bf16[5,32,1536]{2,1,0:T(8,128)(2,1)S(1)}, bf16[5,32,1536]{2,1,0:T(8,128)(2,1)S(1)}, u32[]{:S(2)}, u32[]{:S(2)}) collective-permute-start(bf16[5,32,1536]{2,1,0:T(8,128)(2,1)S(1)} %add_convert_fusion.5), channel_id=1, source_target_pairs={{2,0},{4,2},{6,4},{3,1},{5,3},{7,5},{10,8},{12,10},{14,12},{11,9},... | collective-permute-start | bytes 1474568 | tf_op jit(solution)/shard_map/while/body/eval_jaxpr/ppermute | solution.py:15
  666.1 27.6 %reduce-scatter.7.cloned.1.call-start = ((), (), s32[]{:S(2)}) async-start(), calls=%async_computation.4 | async-start | bytes 1474560 | tf_op jit(solution)/shard_map/while/body/eval_jaxpr/reduce_scatter | solution.py:173
  694.8 15.3 %collective-permute-start.1 = (bf16[5,32,1536]{2,1,0:T(8,128)(2,1)S(1)}, bf16[5,32,1536]{2,1,0:T(8,128)(2,1)S(1)}, u32[]{:S(2)}, u32[]{:S(2)}) collective-permute-start(bf16[5,32,1536]{2,1,0:T(8,128)(2,1)S(1)} %add_convert_fusion.5), channel_id=1, source_target_pairs={{2,0},{4,2},{6,4},{3,1},{5,3},{7,5},{10,8},{12,10},{14,12},{11,9},... | collective-permute-start | bytes 1474568 | tf_op jit(solution)/shard_map/while/body/eval_jaxpr/ppermute | solution.py:15
  710.1 25.7 %reduce-scatter.7.cloned.1.call-start = ((), (), s32[]{:S(2)}) async-start(), calls=%async_computation.4 | async-start | bytes 1474560 | tf_op jit(solution)/shard_map/while/body/eval_jaxpr/reduce_scatter | solution.py:173
  737.0 15.3 %collective-permute-start.1 = (bf16[5,32,1536]{2,1,0:T(8,128)(2,1)S(1)}, bf16[5,32,1536]{2,1,0:T(8,128)(2,1)S(1)}, u32[]{:S(2)}, u32[]{:S(2)}) collective-permute-start(bf16[5,32,1536]{2,1,0:T(8,128)(2,1)S(1)} %add_convert_fusion.5), channel_id=1, source_target_pairs={{2,0},{4,2},{6,4},{3,1},{5,3},{7,5},{10,8},{12,10},{14,12},{11,9},... | collective-permute-start | bytes 1474568 | tf_op jit(solution)/shard_map/while/body/eval_jaxpr/ppermute | solution.py:15
  752.4 27.6 %reduce-scatter.5.cloned.1.call-start = ((), (), s32[]{:S(2)}) async-start(), calls=%async_computation.3 | async-start | bytes 983040
  (4 other events, 3.6 us)
Sparse Core Ops, SparseCore 0:
  9.6 169.4 all-gather.1
  442.7 31.7 reduce-scatter.6
  494.2 23.3 reduce-scatter.6
  537.4 24.2 reduce-scatter.6
  595.9 9.6 reduce-scatter.6
  640.0 9.6 reduce-scatter.6
  684.0 9.6 reduce-scatter.6
  728.0 7.8 reduce-scatter.6
  755.5 24.4 reduce-scatter.4
where the time goes:
time: 837 us; the launch traced here: 835 us
  waiting for transfers between devices  548 us (65%)
  blocking collectives  75.7 us (9%)
  other arithmetic  61 us (7%)
  starting transfers between devices  57.6 us (7%)
  local copies, waits for them, and re-layouts  42.7 us (5%)
  matrix products  34.8 us (4%)
  between operations  13.8 us (2%)
    ppermute x14, waiting for transfers between devices, from_behind(): lax.ppermute(value, axis, [(source, source + steps) for source in range(i...  247 us
    all_gather x1, waiting for transfers between devices, local(): weight = lax.all_gather(weights, 'dp', axis=1, tiled=True)[0]  156 us
    reduce_scatter x7, waiting for transfers between devices, backward_tick(): lax.psum_scatter(grads.astype(jnp.bfloat16), 'mp', scatter_dimension=2, t...  117 us
    ppermute x14, starting transfers between devices, from_behind(): lax.ppermute(value, axis, [(source, source + steps) for source in range(i...  57.5 us
    psum x1, blocking collectives, local(): gram = lax.psum(local_gram, ('dp', 'section'))  40 us
    dot_general x4, matrix products, section_backward(): returned = jnp.dot(flattened, weight.T, preferred_element_type=jnp.float32)  27.5 us
    unnamed x3, waiting for transfers between devices  27.1 us
    all_gather x7, blocking collectives, forward_tick(): joined = lax.all_gather(section_result, 'mp', axis=2, tiled=True)  17.5 us
  transfers between devices with their start and end apart: 23, of which 23 were waited for; matrix products, arithmetic and copies ran while one was open for 0% of the time, Pallas kernels for 0%

commit v1 on v0

v1 whole, which is shorter than its diff:
```python
import functools
import math

import jax
import jax.numpy as jnp
from jax import lax
from jax.experimental import pallas as pl
from jax.experimental.pallas import tpu as pltpu
from jax.sharding import PartitionSpec as P

EPS = 1e-05
ETA = 0.5
MESH = pl.DeviceIdType.MESH
F32 = jnp.float32
BF16 = jnp.bfloat16


def fold(values):
    total = values[..., 0:128]
    for start in range(128, values.shape[-1], 128):
        total = total + values[..., start : start + 128]
    return total


def relay_kernel(
    sections,
    lag_step,
    inputs_ref,
    target_ref,
    gain_ref,
    probe_ref,
    weight_ref,
    acc_ref,
    whole,
    act,
    out,
    cot_in,
    cot_out,
    part_out,
    part_in,
    operand,
    gstack,
    q,
    stats,
    hop_send,
    hop_recv,
    sib_send,
    sib_recv,
    part_send,
    part_recv,
    back_send,
    back_recv,
):
    pos = lax.axis_index("section")
    core = lax.axis_index("mp")
    last = sections - 1
    chunks, tokens, features = inputs_ref.shape
    cols = features // 2
    dirs = probe_ref.shape[1]
    tile = 512 if cols % 512 == 0 else 256 if cols % 256 == 0 else 128
    tiles = cols // tile

    barrier = pltpu.get_barrier_semaphore()
    pl.semaphore_signal(barrier, inc=1, device_id={"mp": 1 - core}, device_id_type=MESH)

    @pl.when(pos > 0)
    def _():
        pl.semaphore_signal(barrier, inc=1, device_id={"section": pos - 1}, device_id_type=MESH)

    @pl.when(pos < last)
    def _():
        pl.semaphore_signal(barrier, inc=1, device_id={"section": pos + 1}, device_id_type=MESH)

    peers = 1 + (pos > 0).astype(jnp.int32) + (pos < last).astype(jnp.int32)
    pl.semaphore_wait(barrier, peers)

    def hop(c):
        return pltpu.make_async_remote_copy(
            src_ref=out.at[c],
            dst_ref=whole.at[c, core],
            send_sem=hop_send.at[c],
            recv_sem=hop_recv.at[c],
            device_id={"section": pos + 1},
            device_id_type=MESH,
        )

    def sibling(c):
        return pltpu.make_async_remote_copy(
            src_ref=whole.at[c, core],
            dst_ref=whole.at[c, core],
            send_sem=sib_send.at[c],
            recv_sem=sib_recv.at[c],
            device_id={"mp": 1 - core},
            device_id_type=MESH,
        )

    def part(c):
        return pltpu.make_async_remote_copy(
            src_ref=part_out.at[c],
            dst_ref=part_in.at[c],
            send_sem=part_send.at[c],
            recv_sem=part_recv.at[c],
            device_id={"mp": 1 - core},
            device_id_type=MESH,
        )

    def back(c):
        return pltpu.make_async_remote_copy(
            src_ref=cot_out.at[c],
            dst_ref=cot_in.at[c],
            send_sem=back_send.at[c],
            recv_sem=back_recv.at[c],
            device_id={"section": pos - 1},
            device_id_type=MESH,
        )

    def rows(k):
        return pl.ds(k * tokens, tokens)

    acc_ref[...] = jnp.zeros_like(acc_ref)

    def forward(c):
        @pl.when(pos == 0)
        def _():
            for half in range(2):
                whole[c, half, 0:tokens, :] = inputs_ref[c, :, half * cols : (half + 1) * cols]
                whole[c, half, tokens:, :] = jnp.zeros((dirs * tokens, cols), BF16)

        @pl.when(pos > 0)
        def _():
            hop(c).wait_recv()
            swap = sibling(c)
            swap.start()
            swap.wait_recv()

        square = jnp.zeros((tokens, 128), F32)
        cross = [jnp.zeros((tokens, 128), F32) for _ in range(dirs)]
        for half in range(2):
            for j in range(tiles):
                at = pl.ds(j * tile, tile)
                h = whole[c, half, rows(0), at].astype(F32)
                square = square + fold(h * h)
                for k in range(dirs):
                    cross[k] = cross[k] + fold(h * whole[c, half, rows(k + 1), at].astype(F32))
        s = lax.rsqrt(jnp.sum(square, axis=-1, keepdims=True) / features + EPS)
        cube = -(s * s * s) / features
        u = [cube * jnp.sum(cross[k], axis=-1, keepdims=True) for k in range(dirs)]
        stats[c, 0] = jnp.broadcast_to(s, (tokens, 128))
        for k in range(dirs):
            stats[c, k + 1] = jnp.broadcast_to(u[k], (tokens, 128))
        for half in range(2):
            for j in range(tiles):
                at = pl.ds(j * tile, tile)
                h = whole[c, half, rows(0), at].astype(F32)
                gain = gain_ref[half, :, at]
                n = h * s
                operand[half, rows(0), at] = (n * gain).astype(BF16)
                for k in range(dirs):
                    t = whole[c, half, rows(k + 1), at].astype(F32)
                    mixed = (t * s + h * u[k]) * gain + n * probe_ref[half, k : k + 1, at]
                    operand[half, rows(k + 1), at] = mixed.astype(BF16)

        def product(j, carry):
            at = pl.ds(pl.multiple_of(j * tile, tile), tile)
            a = jnp.dot(operand[0], weight_ref[0, :, at], preferred_element_type=F32)
            a = a + jnp.dot(operand[1], weight_ref[1, :, at], preferred_element_type=F32)
            b = jnp.tanh(a[0:tokens])
            slope = 1.0 - b * b
            act[c, rows(0), at] = b
            out[c, rows(0), at] = (whole[c, core, rows(0), at].astype(F32) + b).astype(BF16)
            for k in range(1, dirs + 1):
                bk = slope * a[k * tokens : (k + 1) * tokens]
                act[c, rows(k), at] = bk
                out[c, rows(k), at] = (whole[c, core, rows(k), at].astype(F32) + bk).astype(BF16)
            return carry

        lax.fori_loop(0, tiles, product, 0)

        @pl.when(pos < last)
        def _():
            hop(c).start()

    def backward(c):
        @pl.when(pos == last)
        def _():
            error = out[c, rows(0), :].astype(F32) - target_ref[c].astype(F32)
            cot_in[c, rows(0), :] = error.astype(BF16)
            cot_in[c, tokens:, :] = out[c, tokens:, :]

        @pl.when(pos < last)
        def _():
            back(c).wait_recv()

        for j in range(tiles):
            at = pl.ds(j * tile, tile)
            c0 = cot_in[c, rows(0), at].astype(F32)
            b = act[c, rows(0), at]
            slope = 1.0 - b * b
            twice = 2.0 * b * c0
            gstack[rows(0), at] = (c0 * slope).astype(BF16)
            for k in range(1, dirs + 1):
                ck = cot_in[c, rows(k), at].astype(F32)
                gstack[rows(k), at] = (ck * slope - twice * act[c, rows(k), at]).astype(BF16)

        s = stats[c, 0, :, 0:1]
        u = [stats[c, k + 1, :, 0:1] for k in range(dirs)]

        def product(j, sums):
            half = j // tiles
            at = pl.ds(pl.multiple_of((j % tiles) * tile, tile), tile)
            q_all = lax.dot_general(
                gstack[...],
                weight_ref[half, at, :],
                (((1,), (1,)), ((), ())),
                preferred_element_type=F32,
            )
            q[half, :, at] = q_all
            h = whole[c, half, rows(0), at].astype(F32)
            gain = gain_ref[half, :, at]
            q0 = q_all[0:tokens]
            n = h * s
            p = q0 * gain
            new = [sums[0] + fold(p * h)]
            for k in range(dirs):
                t = whole[c, half, rows(k + 1), at].astype(F32)
                qk = q_all[(k + 1) * tokens : (k + 2) * tokens]
                v = t * s + h * u[k]
                pk = qk * gain + q0 * probe_ref[half, k : k + 1, at]
                new.append(sums[k + 1] + fold(pk * h + p * t))
                acc_ref[half, k : k + 1, at] += jnp.sum(qk * n + q0 * v, axis=0, keepdims=True)
            return tuple(new)

        zero = jnp.zeros((tokens, 128), F32)
        sums = lax.fori_loop(0, 2 * tiles, product, (zero,) * (dirs + 1))

        @pl.when(pos > 0)
        def _():
            w = [jnp.sum(value, axis=-1, keepdims=True) for value in sums]
            cube = s * s * s / features
            w0 = cube * w[0]
            pull = [(3.0 / features) * s * s * u[k] * w[0] + cube * w[k + 1] for k in range(dirs)]

            def leaving(half, at):
                h = whole[c, half, rows(0), at].astype(F32)
                gain = gain_ref[half, :, at]
                q0 = q[half, rows(0), at]
                p = q0 * gain
                yield s * p - h * w0
                for k in range(dirs):
                    t = whole[c, half, rows(k + 1), at].astype(F32)
                    pk = q[half, rows(k + 1), at] * gain + q0 * probe_ref[half, k : k + 1, at]
                    yield u[k] * p + s * pk - h * pull[k] - t * w0

            for j in range(tiles):
                at = pl.ds(j * tile, tile)
                for k, value in enumerate(leaving(1 - core, at)):
                    part_out[c, rows(k), at] = value.astype(BF16)
            exchange = part(c)
            exchange.start()
            for j in range(tiles):
                at = pl.ds(j * tile, tile)
                for k, value in enumerate(list(leaving(core, at))):
                    q[core, rows(k), at] = value + cot_in[c, rows(k), at].astype(F32)
            exchange.wait_recv()
            for j in range(tiles):
                at = pl.ds(j * tile, tile)
                cot_out[c, :, at] = (q[core, :, at] + part_in[c, :, at].astype(F32)).astype(BF16)
            back(c).start()

    lag = jnp.minimum(lag_step * (last - pos), chunks)

    def turn(i, carry):
        @pl.when(i < chunks)
        def _():
            forward(jnp.minimum(i, chunks - 1))

        @pl.when((i >= lag) & (i - lag < chunks))
        def _():
            backward(jnp.clip(i - lag, 0, chunks - 1))

        return carry

    lax.fori_loop(0, chunks + min(lag_step * last, chunks), turn, 0)

    def drain(c, carry):
        @pl.when(pos < last)
        def _():
            hop(c).wait_send()

        @pl.when(pos > 0)
        def _():
            sibling(c).wait_send()
            part(c).wait_send()
            back(c).wait_send()

        return carry

    lax.fori_loop(0, chunks, drain, 0)


def relay(inputs, target, gain, probe, weight, sections, chunk_tokens, lag_step):
    features = inputs.shape[-1]
    cols = features // 2
    dirs = probe.shape[0]
    chunks = inputs.shape[0] * inputs.shape[1] // chunk_tokens
    height = (dirs + 1) * chunk_tokens
    vmem = pl.BlockSpec(memory_space=pltpu.VMEM)
    dma = pltpu.SemaphoreType.DMA((chunks,))
    acc = pl.pallas_call(
        functools.partial(relay_kernel, sections, lag_step),
        out_shape=jax.ShapeDtypeStruct((2, dirs, cols), F32),
        in_specs=[vmem] * 5,
        out_specs=vmem,
        scratch_shapes=[
            pltpu.VMEM((chunks, 2, height, cols), BF16),
            pltpu.VMEM((chunks, height, cols), F32),
            pltpu.VMEM((chunks, height, cols), BF16),
            pltpu.VMEM((chunks, height, cols), BF16),
            pltpu.VMEM((chunks, height, cols), BF16),
            pltpu.VMEM((chunks, height, cols), BF16),
            pltpu.VMEM((chunks, height, cols), BF16),
            pltpu.VMEM((2, height, cols), BF16),
            pltpu.VMEM((height, cols), BF16),
            pltpu.VMEM((2, height, cols), F32),
            pltpu.VMEM((chunks, dirs + 1, chunk_tokens, 128), F32),
        ]
        + [dma] * 8,
        compiler_params=pltpu.CompilerParams(
            collective_id=0, has_side_effects=True, vmem_limit_bytes=56 * 1024 * 1024
        ),
        cost_estimate=pl.CostEstimate(
            flops=4 * chunks * height * features * cols, bytes_accessed=2 * features * cols, transcendentals=0
        ),
    )(
        inputs.reshape(chunks, chunk_tokens, features),
        target.reshape(chunks, chunk_tokens, cols),
        gain.reshape(2, 1, cols),
        probe.reshape(dirs, 2, cols).transpose(1, 0, 2),
        weight.reshape(2, cols, cols),
    )
    return acc.transpose(1, 0, 2).reshape(dirs, features)


def local(inputs, target, gains, weights, probes):
    sections = lax.axis_size("section")
    batches, micro_batch_tokens, features = inputs.shape
    weight = lax.all_gather(weights, "dp", axis=1, tiled=True)[0]
    probe_dirs = lax.all_gather(probes.astype(BF16), "dp", axis=2, tiled=True).astype(F32)[:, 0, :]
    accumulated = relay(inputs, target, gains[0], probe_dirs, weight, sections, 16, 3)
    divisor = batches * micro_batch_tokens * lax.axis_size("dp")
    own_probe = probes[:, 0, :]
    owned = lax.psum_scatter(
        accumulated.astype(BF16), "dp", scatter_dimension=1, tiled=True
    ).astype(F32)
    owned = lax.psum(owned, "mp")
    curvature = owned / divisor
    moved = own_probe + ETA * curvature
    local_gram = jnp.dot(moved, moved.T, precision=lax.Precision.HIGHEST)
    gram = lax.psum(local_gram, ("dp", "section"))
    factor = jnp.linalg.cholesky(gram)
    rotated = jax.scipy.linalg.solve_triangular(factor, moved, lower=True) * math.sqrt(
        sections * features
    )
    return (curvature[:, None, :], rotated[:, None, :])


def solution(mesh):
    in_specs = (
        P(None, "dp", None),
        P(None, "dp", "mp"),
        P("section", None),
        P("section", "dp", "mp"),
        P(None, "section", "dp"),
    )
    out_specs = (P(None, "section", "dp"), P(None, "section", "dp"))
    return jax.shard_map(local, mesh=mesh, in_specs=in_specs, out_specs=out_specs, check_vma=False)
```

time: 837 us -> 407 us (0.49)
  waiting for transfers between devices: 548 us -> 175 us
  Pallas kernels: 0 us -> 150 us
  starting transfers between devices: 57.6 us -> 0.08 us
  other arithmetic: 61 us -> 4.31 us
  local copies, waits for them, and re-layouts: 42.7 us -> 3.57 us
  matrix products: 34.8 us -> 0.38 us
  blocking collectives: 75.7 us -> 58.2 us
    ppermute x14 -> x0, waiting for transfers between devices: 247 us -> none  [from_behind(): lax.ppermute(value, axis, [(source, source + steps) for source in range(i...]
    pallas_call x0 -> x1, Pallas kernels: none -> 150 us  [relay(): pl.pallas_call(functools.partial(relay_kernel, sections, lag_step), out_s...]
    reduce_scatter x7 -> x0, waiting for transfers between devices: 117 us -> none  [backward_tick(): lax.psum_scatter(grads.astype(jnp.bfloat16), 'mp', scatter_dimension=2, t...]
    ppermute x14 -> x0, starting transfers between devices: 57.5 us -> none  [from_behind(): lax.ppermute(value, axis, [(source, source + steps) for source in range(i...]
    dot_general x8 -> x0, matrix products: 34.4 us -> none  [the longest x4 27.5 us: section_backward(): returned = jnp.dot(flattened, weight.T, preferred_element_type=jnp.float32)]
    convert_element_type x28 -> x2, other arithmetic: 21.6 us -> 1.53 us  [the longest x1 0.81 us: local(): accumulated.astype(BF16)]
    all_gather x8 -> x1, blocking collectives: 32.3 us -> 14.8 us  [local(): lax.all_gather(probes.astype(BF16), 'dp', axis=2, tiled=True).astype(F32)]
    another operation x16 -> x0, other arithmetic: 11.3 us -> none
  transfers between devices with their start and end apart: 23 -> 2, of which waited for: 23 -> 2; matrix products, arithmetic and copies ran while one was open for 0% -> 0% of each run, Pallas kernels for 0% -> 0%
where the time goes in v1:
time: 407 us; the launch traced here: 406 us
  waiting for transfers between devices  175 us (43%)
  Pallas kernels  150 us (37%)
  blocking collectives  58.2 us (14%)
  between operations  14.1 us (3%)
  other arithmetic  4.31 us (1%)
    all_gather x1, waiting for transfers between devices, local(): weight = lax.all_gather(weights, 'dp', axis=1, tiled=True)[0]  155 us
    pallas_call x1, Pallas kernels, relay(): pl.pallas_call(functools.partial(relay_kernel, sections, lag_step), out_s...  150 us
    psum x1, blocking collectives, local(): gram = lax.psum(local_gram, ('dp', 'section'))  40.1 us
    unnamed x3, waiting for transfers between devices  20.6 us
    all_gather x1, blocking collectives, local(): lax.all_gather(probes.astype(BF16), 'dp', axis=2, tiled=True).astype(F32)  14.8 us
  transfers between devices with their start and end apart: 2, of which 2 were waited for; matrix products, arithmetic and copies ran while one was open for 0% of the time, Pallas kernels for 0%

profile of v1, /device:TPU:0, one launch (start us, length us, event | category | flops | bytes accessed | tf_op | source)
XLA Modules:
  0.0 406.3 jit_solution(577283398403282023)
XLA Ops:
  7.2 0.0 all-gather.2.cloned.1.call-start
  7.2 0.7 all-gather.2.cloned.1.call-update
  7.9 0.0 reduce-scatter.4.cloned.1.call-start
  7.9 0.7 convert_element_type.16
  8.7 14.8 %all_gather.6 = bf16[4,1,3072]{2,1,0:T(2,128)(2,1)S(1)} all-gather(bf16[4,1,768]{2,1,0:T(2,128)(2,1)S(1)} %convert_element_type.16), channel_id=1, replica_groups=mesh['dp'=4,'section'=4,'mp'=2] {'dp'}, dimensions={2}, use_global_device_ids=true | all-gather | bytes 30720 | tf_op jit(solution)/shard_map/all_gather | solution.py:348
  23.4 0.8 convert_reduce_fusion
  24.2 154.9 %all-gather.2.cloned.1.call-done = bf16[1,3072,1536]{2,1,0:T(8,128)(2,1)} async-done(((bf16[1,768,1536]{2,1,0:T(8,128)(2,1)}), bf16[1,3072,1536]{2,1,0:T(8,128)(2,1)}) %all-gather.2.cloned.1.call-update) | async-done | bytes 9437200 | tf_op jit(solution)/shard_map/all_gather | solution.py:347
  179.1 0.0 copy-start
  179.1 150.3 %shard_map.68 = f32[2,4,1536]{2,1,0:T(4,128)} custom-call(bf16[8,16,3072]{2,1,0:T(8,128)(2,1)} %bitcast.35, bf16[8,16,1536]{2,1,0:T(8,128)(2,1)} %bitcast.36, f32[2,1,1536]{2,1,0:T(1,128)} %bitcast.37, f32[2,4,1536]{2,1,0:T(4,128)} %bitcast.33, bf16[2,1536,1536]{2,1,0:T(8,128)(2,1)} %bitcast.34), custom_call_target="tpu_custom_call" | custom-call | flops 12079595520 | bytes 9437184 | tf_op jit(solution)/shard_map/pallas_call | solution.py:309
  329.4 0.8 convert_element_type.17
  330.2 1.2 copy.23
  331.4 0.0 reduce-scatter.4.cloned.1.call-update
  331.4 19.9 %reduce-scatter.4.cloned.1.call-done = bf16[768,4]{1,0:T(8,128)(2,1)} async-done(((bf16[3072,4]{1,0:T(8,128)(2,1)}), bf16[768,4]{1,0:T(8,128)(2,1)}) %reduce-scatter.4.cloned.1.call-update) | async-done | bytes 6160
  351.3 1.0 copy.24
  352.3 3.3 psum.14
  355.7 0.0 copy-done
  355.7 0.1 fusion.4
  355.8 40.1 %psum.15 = f32[4,4]{0,1:T(4,128)S(1)} all-reduce(f32[4,4]{0,1:T(4,128)S(1)} %fusion.4), channel_id=1, replica_groups=mesh['dp'=4,'section'=4,'mp'=2] {'dp','section'}, use_global_device_ids=true, to_apply=%region_2.0 | all-reduce | flops 16 | bytes 128 | tf_op jit(solution)/shard_map/psum | solution.py:359
  395.9 0.1 copy.18
  396.0 0.4 cholesky.16
  396.4 0.6 compare_reduce_fusion
  397.0 0.6 fusion.1
  397.7 0.3 custom-call.7
  398.0 0.2 fusion
  398.3 0.6 copy.20
  398.9 0.6 copy.21
  (3 shorter events, 0.0 us)
Async XLA Ops:
  7.2 171.9 %all-gather.2.cloned.1.call-start = ((), (), s32[]{:S(2)}) async-start(), calls=%async_computation.1 | async-start | bytes 11796480 | tf_op jit(solution)/shard_map/all_gather | solution.py:347
  7.9 343.4 %reduce-scatter.4.cloned.1.call-start = ((), (), s32[]{:S(2)}) async-start(), calls=%async_computation.2 | async-start | bytes 983040
  179.1 176.6 %copy-start = (f32[4,1,768]{2,1,0:T(1,128)S(1)}, f32[4,1,768]{2,1,0:T(1,128)}, u32[]{:S(2)}) copy-start(f32[4,1,768]{2,1,0:T(1,128)} %param.9) | copy-start | bytes 36868
Sparse Core Ops, SparseCore 0:
  9.6 169.4 all-gather.1
  331.6 19.6 reduce-scatter.3

commit v2 on v1

--- a/solution.py
+++ b/solution.py
@@ -28,9 +28,11 @@
     inputs_ref,
     target_ref,
     gain_ref,
-    probe_ref,
-    weight_ref,
+    probe_block_ref,
+    weight_block_ref,
     acc_ref,
+    weight_all,
+    probe_all,
     whole,
     act,
     out,
@@ -50,13 +52,25 @@
     part_recv,
     back_send,
     back_recv,
+    right_send,
+    right_recv,
+    left_send,
+    left_recv,
+    probe_send,
+    probe_recv,
+    own_sem,
 ):
     pos = lax.axis_index("section")
     core = lax.axis_index("mp")
     last = sections - 1
     chunks, tokens, features = inputs_ref.shape
     cols = features // 2
-    dirs = probe_ref.shape[1]
+    dirs = probe_all.shape[0]
+    owners = lax.axis_size("dp")
+    me = lax.axis_index("dp")
+    depth = weight_block_ref.shape[0]
+    width = probe_block_ref.shape[1]
+    gather_probes = width < features
     tile = 512 if cols % 512 == 0 else 256 if cols % 256 == 0 else 128
     tiles = cols // tile
 
@@ -71,8 +85,70 @@
     def _():
         pl.semaphore_signal(barrier, inc=1, device_id={"section": pos + 1}, device_id_type=MESH)
 
-    peers = 1 + (pos > 0).astype(jnp.int32) + (pos < last).astype(jnp.int32)
+    def block_rows(b):
+        return pl.ds(pl.multiple_of(b * depth, depth), depth)
+
+    def greet(step, carry):
+        peer = lax.rem(me + step, owners)
+        pl.semaphore_signal(barrier, inc=1, device_id={"dp": peer}, device_id_type=MESH)
+        return carry
+
+    lax.fori_loop(1, owners, greet, 0)
+    own = pltpu.make_async_copy(weight_block_ref, weight_all.at[block_rows(me)], own_sem)
+    own.start()
+    peers = owners + (pos > 0).astype(jnp.int32) + (pos < last).astype(jnp.int32)
     pl.semaphore_wait(barrier, peers)
+    own.wait()
+
+    def to_right(b):
+        return pltpu.make_async_remote_copy(
+            src_ref=weight_all.at[block_rows(b)],
+            dst_ref=weight_all.at[block_rows(b)],
+            send_sem=right_send.at[b],
+            recv_sem=right_recv.at[b],
+            device_id={"dp": me + 1},
+            device_id_type=MESH,
+        )
+
+    def to_left(b):
+        return pltpu.make_async_remote_copy(
+            src_ref=weight_all.at[block_rows(b)],
+            dst_ref=weight_all.at[block_rows(b)],
+            send_sem=left_send.at[b],
+            recv_sem=left_recv.at[b],
+            device_id={"dp": me - 1},
+            device_id_type=MESH,
+        )
+
+    @pl.when(me < owners - 1)
+    def _():
+        to_right(me).start()
+
+    @pl.when(me > 0)
+    def _():
+        to_left(me).start()
+
+    def probe_to(step):
+        mine = pl.ds(pl.multiple_of(me * width, width), width)
+        return pltpu.make_async_remote_copy(
+            src_ref=probe_all.at[:, mine],
+            dst_ref=probe_all.at[:, mine],
+            send_sem=probe_send.at[step],
+            recv_sem=probe_recv.at[step],
+            device_id={"dp": lax.rem(me + step, owners)},
+            device_id_type=MESH,
+        )
+
+    if gather_probes:
+        probe_all[:, pl.ds(pl.multiple_of(me * width, width), width)] = probe_block_ref[...]
+
+        def spread(step, carry):
+            probe_to(step).start()
+            return carry
+
+        lax.fori_loop(1, owners, spread, 0)
+    else:
+        probe_all[...] = probe_block_ref[...]
 
     def hop(c):
         return pltpu.make_async_remote_copy(
@@ -114,10 +190,46 @@
             device_id_type=MESH,
         )
 
+    def probe_at(half, k, at):
+        start = half * cols + at.start
+        if not isinstance(start, int):
+            start = pl.multiple_of(start, 128)
+        return probe_all[k : k + 1, pl.ds(start, tile)]
+
     def rows(k):
         return pl.ds(k * tokens, tokens)
 
     acc_ref[...] = jnp.zeros_like(acc_ref)
+
+    def relay_blocks(step, carry):
+        low, high = me - step, me + step
+
+        @pl.when(low >= 0)
+        def _():
+            to_right(low).wait_recv()
+
+            @pl.when(me < owners - 1)
+            def _():
+                to_right(low).start()
+
+        @pl.when(high < owners)
+        def _():
+            to_left(high).wait_recv()
+
+            @pl.when(me > 0)
+            def _():
+                to_left(high).start()
+
+        return carry
+
+    lax.fori_loop(1, owners, relay_blocks, 0)
+    if gather_probes:
+
+        def probes_in(step, carry):
+            probe_to(step).wait_recv()
+            return carry
+
+        lax.fori_loop(1, owners, probes_in, 0)
 
     def forward(c):
         @pl.when(pos == 0)
@@ -157,13 +269,13 @@
                 operand[half, rows(0), at] = (n * gain).astype(BF16)
                 for k in range(dirs):
                     t = whole[c, half, rows(k + 1), at].astype(F32)
-                    mixed = (t * s + h * u[k]) * gain + n * probe_ref[half, k : k + 1, at]
+                    mixed = (t * s + h * u[k]) * gain + n * probe_at(half, k, at)
                     operand[half, rows(k + 1), at] = mixed.astype(BF16)
 
         def product(j, carry):
             at = pl.ds(pl.multiple_of(j * tile, tile), tile)
-            a = jnp.dot(operand[0], weight_ref[0, :, at], preferred_element_type=F32)
-            a = a + jnp.dot(operand[1], weight_ref[1, :, at], preferred_element_type=F32)
+            a = jnp.dot(operand[0], weight_all[0:cols, at], preferred_element_type=F32)
+            a = a + jnp.dot(operand[1], weight_all[cols:, at], preferred_element_type=F32)
             b = jnp.tanh(a[0:tokens])
             slope = 1.0 - b * b
             act[c, rows(0), at] = b
@@ -210,7 +322,7 @@
             at = pl.ds(pl.multiple_of((j % tiles) * tile, tile), tile)
             q_all = lax.dot_general(
                 gstack[...],
-                weight_ref[half, at, :],
+                weight_all[pl.ds(pl.multiple_of(j * tile, tile), tile), :],
                 (((1,), (1,)), ((), ())),
                 preferred_element_type=F32,
             )
@@ -225,7 +337,7 @@
                 t = whole[c, half, rows(k + 1), at].astype(F32)
                 qk = q_all[(k + 1) * tokens : (k + 2) * tokens]
                 v = t * s + h * u[k]
-                pk = qk * gain + q0 * probe_ref[half, k : k + 1, at]
+                pk = qk * gain + q0 * probe_at(half, k, at)
                 new.append(sums[k + 1] + fold(pk * h + p * t))
                 acc_ref[half, k : k + 1, at] += jnp.sum(qk * n + q0 * v, axis=0, keepdims=True)
             return tuple(new)
@@ -248,7 +360,7 @@
                 yield s * p - h * w0
                 for k in range(dirs):
                     t = whole[c, half, rows(k + 1), at].astype(F32)
-                    pk = q[half, rows(k + 1), at] * gain + q0 * probe_ref[half, k : k + 1, at]
+                    pk = q[half, rows(k + 1), at] * gain + q0 * probe_at(half, k, at)
                     yield u[k] * p + s * pk - h * pull[k] - t * w0
 
             for j in range(tiles):
@@ -297,6 +409,165 @@
 
     lax.fori_loop(0, chunks, drain, 0)
 
+    def drain_blocks(b, carry):
+        @pl.when((me < owners - 1) & (b <= me))
+        def _():
+            to_right(b).wait_send()
+
+        @pl.when((me > 0) & (b >= me))
+        def _():
+            to_left(b).wait_send()
+
+        return carry
+
+    lax.fori_loop(0, owners, drain_blocks, 0)
+    if gather_probes:
+
+        def drain_probes(step, carry):
+            probe_to(step).wait_send()
+            return carry
+
+        lax.fori_loop(1, owners, drain_probes, 0)
+
+
+def settle_kernel(scale, divisor, parts_ref, probe_ref, hvp_ref, next_ref, got, tiles, sends, recvs, tile_sends, tile_recvs):
+    owners, dirs, width = parts_ref.shape
+    sections = lax.axis_size("section")
+    dp, pos, core = lax.axis_index("dp"), lax.axis_index("section"), lax.axis_index("mp")
+    pairs = [(i, j) for i in range(dirs) for j in range(i + 1)]
+    group = 2 * owners
+    everyone = owners * sections
+    me = dp * 2 + core
+    place = dp * sections + pos
+
+    barrier = pltpu.get_barrier_semaphore()
+
+    def greet_owner(step, carry):
+        peer = lax.rem(me + step, group)
+        target = {"dp": peer // 2, "mp": lax.rem(peer, 2)}
+        pl.semaphore_signal(barrier, inc=1, device_id=target, device_id_type=MESH)
+        return carry
+
+    def greet_other(step, carry):
+        target = {"dp": lax.rem(step, owners), "section": lax.rem(pos + 1 + step // owners, sections)}
+        pl.semaphore_signal(barrier, inc=1, device_id=target, device_id_type=MESH)
+        return carry
+
+    lax.fori_loop(1, group, greet_owner, 0)
+    lax.fori_loop(0, owners * (sections - 1), greet_other, 0)
+    pl.semaphore_wait(barrier, group - 1 + owners * (sections - 1))
+
+    def give(step):
+        peer = lax.rem(me + step, group)
+        return pltpu.make_async_remote_copy(
+            src_ref=parts_ref.at[peer // 2],
+            dst_ref=got.at[step],
+            send_sem=sends.at[step],
+            recv_sem=recvs.at[step],
+            device_id={"dp": peer // 2, "mp": lax.rem(peer, 2)},
+            device_id_type=MESH,
+        )
+
+    def start_give(step, carry):
+        give(step).start()
+        return carry
+
+    lax.fori_loop(1, group, start_give, 0)
+
+    def take(step, total):
+        give(step).wait_recv()
+        return total + got[step]
+
+    curvature = lax.fori_loop(1, group, take, parts_ref[dp]) / divisor
+    hvp_ref[...] = curvature
+    moved = probe_ref[...] + ETA * curvature
+    row = lax.broadcasted_iota(jnp.int32, (16, 128), 0)
+    tile = jnp.zeros((16, 128), F32)
+    for index, (i, j) in enumerate(pairs):
+        inner = jnp.sum(moved[i : i + 1] * moved[j : j + 1], axis=1, keepdims=True)
+        tile = jnp.where(row == index, inner, tile)
+    tiles[0] = tile
+
+    def tell(step):
+        peer = lax.rem(place + step, everyone)
+        return pltpu.make_async_remote_copy(
+            src_ref=tiles.at[0],
+            dst_ref=tiles.at[step],
+            send_sem=tile_sends.at[step],
+            recv_sem=tile_recvs.at[step],
+            device_id={"dp": peer // sections, "section": lax.rem(peer, sections)},
+            device_id_type=MESH,
+        )
+
+    def start_tell(step, carry):
+        tell(step).start()
+        return carry
+
+    lax.fori_loop(1, everyone, start_tell, 0)
+
+    def hear(step, carry):
+        tell(step).wait_recv()
+        return carry
+
+    lax.fori_loop(1, everyone, hear, 0)
+    gram = lax.fori_loop(
+        0,
+        everyone,
+        lambda source, total: total + tiles[lax.rem(place - source + everyone, everyone)],
+        jnp.zeros((16, 128), F32),
+    )
+    entry = {pair: gram[index : index + 1, 0:1] for index, pair in enumerate(pairs)}
+    factor = {}
+    for j in range(dirs):
+        rest = entry[j, j]
+        for k in range(j):
+            rest = rest - factor[j, k] * factor[j, k]
+        factor[j, j] = jnp.sqrt(rest)
+        for i in range(j + 1, dirs):
+            rest = entry[i, j]
+            for k in range(j):
+                rest = rest - factor[i, k] * factor[j, k]
+            factor[i, j] = rest / factor[j, j]
+    solved = []
+    for i in range(dirs):
+        value = moved[i : i + 1]
+        for k in range(i):
+            value = value - factor[i, k] * solved[k]
+        solved.append(value / factor[i, i])
+        next_ref[i : i + 1, :] = solved[i] * scale
+
+    def drain_give(step, carry):
+        give(step).wait_send()
+        return carry
+
+    def drain_tell(step, carry):
+        tell(step).wait_send()
+        return carry
+
+    lax.fori_loop(1, group, drain_give, 0)
+    lax.fori_loop(1, everyone, drain_tell, 0)
+
+
+def settle(accumulated, own_probe, scale, divisor):
+    dirs, width = own_probe.shape
+    owners, sections = lax.axis_size("dp"), lax.axis_size("section")
+    vmem = pl.BlockSpec(memory_space=pltpu.VMEM)
+    return pl.pallas_call(
+        functools.partial(settle_kernel, scale, divisor),
+        out_shape=[jax.ShapeDtypeStruct((dirs, width), F32)] * 2,
+        in_specs=[vmem] * 2,
+        out_specs=[vmem] * 2,
+        scratch_shapes=[
+            pltpu.VMEM((2 * owners, dirs, width), F32),
+            pltpu.VMEM((owners * sections, 16, 128), F32),
+        ]
+        + [pltpu.SemaphoreType.DMA((2 * owners,))] * 2
+        + [pltpu.SemaphoreType.DMA((owners * sections,))] * 2,
+        compiler_params=pltpu.CompilerParams(
+            collective_id=1, has_side_effects=True, vmem_limit_bytes=16 * 1024 * 1024
+        ),
+    )(accumulated.reshape(dirs, owners, width).transpose(1, 0, 2), own_probe)
+
 
 def relay(inputs, target, gain, probe, weight, sections, chunk_tokens, lag_step):
     features = inputs.shape[-1]
@@ -306,12 +577,15 @@
     height = (dirs + 1) * chunk_tokens
     vmem = pl.BlockSpec(memory_space=pltpu.VMEM)
     dma = pltpu.SemaphoreType.DMA((chunks,))
+    ring = pltpu.SemaphoreType.DMA((lax.axis_size("dp"),))
     acc = pl.pallas_call(
         functools.partial(relay_kernel, sections, lag_step),
         out_shape=jax.ShapeDtypeStruct((2, dirs, cols), F32),
-        in_specs=[vmem] * 5,
+        in_specs=[vmem] * 4 + [pl.BlockSpec(memory_space=pl.ANY)],
         out_specs=vmem,
         scratch_shapes=[
+            pltpu.VMEM((features, cols), BF16),
+            pltpu.VMEM((dirs, features), F32),
             pltpu.VMEM((chunks, 2, height, cols), BF16),
             pltpu.VMEM((chunks, height, cols), F32),
             pltpu.VMEM((chunks, height, cols), BF16),
@@ -324,7 +598,9 @@
             pltpu.VMEM((2, height, cols), F32),
             pltpu.VMEM((chunks, dirs + 1, chunk_tokens, 128), F32),
         ]
-        + [dma] * 8,
+        + [dma] * 8
+        + [ring] * 6
+        + [pltpu.SemaphoreType.DMA],
         compiler_params=pltpu.CompilerParams(
             collective_id=0, has_side_effects=True, vmem_limit_bytes=56 * 1024 * 1024
         ),
@@ -335,8 +611,8 @@
         inputs.reshape(chunks, chunk_tokens, features),
         target.reshape(chunks, chunk_tokens, cols),
         gain.reshape(2, 1, cols),
-        probe.reshape(dirs, 2, cols).transpose(1, 0, 2),
-        weight.reshape(2, cols, cols),
+        probe,
+        weight,
     )
     return acc.transpose(1, 0, 2).reshape(dirs, features)
 
@@ -344,23 +620,12 @@
 def local(inputs, target, gains, weights, probes):
     sections = lax.axis_size("section")
     batches, micro_batch_tokens, features = inputs.shape
-    weight = lax.all_gather(weights, "dp", axis=1, tiled=True)[0]
-    probe_dirs = lax.all_gather(probes.astype(BF16), "dp", axis=2, tiled=True).astype(F32)[:, 0, :]
-    accumulated = relay(inputs, target, gains[0], probe_dirs, weight, sections, 16, 3)
+    probe_block = probes[:, 0, :]
+    if probe_block.shape[1] % 128:
+        probe_block = lax.all_gather(probe_block, "dp", axis=1, tiled=True)
+    accumulated = relay(inputs, target, gains[0], probe_block, weights[0], sections, 16, 3)
     divisor = batches * micro_batch_tokens * lax.axis_size("dp")
-    own_probe = probes[:, 0, :]
-    owned = lax.psum_scatter(
-        accumulated.astype(BF16), "dp", scatter_dimension=1, tiled=True
-    ).astype(F32)
-    owned = lax.psum(owned, "mp")
-    curvature = owned / divisor
-    moved = own_probe + ETA * curvature
-    local_gram = jnp.dot(moved, moved.T, precision=lax.Precision.HIGHEST)
-    gram = lax.psum(local_gram, ("dp", "section"))
-    factor = jnp.linalg.cholesky(gram)
-    rotated = jax.scipy.linalg.solve_triangular(factor, moved, lower=True) * math.sqrt(
-        sections * features
-    )
+    curvature, rotated = settle(accumulated, probes[:, 0, :], math.sqrt(sections * features), divisor)
     return (curvature[:, None, :], rotated[:, None, :])
 
 

time: 407 us -> 322 us (0.79)
  waiting for transfers between devices: 175 us -> 0 us
  Pallas kernels: 150 us -> 318 us
  blocking collectives: 58.2 us -> 0 us
  between operations: 14.1 us -> 0.66 us
  other arithmetic: 4.31 us -> 0 us
    pallas_call x1, Pallas kernels: 150 us -> 306 us  [relay(): pl.pallas_call(functools.partial(relay_kernel, sections, lag_step), out_s...]
    all_gather x1 -> x0, waiting for transfers between devices: 155 us -> none  [local(): weight = lax.all_gather(weights, 'dp', axis=1, tiled=True)[0]]
    psum x2 -> x0, blocking collectives: 43.4 us -> none  [the longest x1 40.1 us: local(): gram = lax.psum(local_gram, ('dp', 'section'))]
    unnamed x3 -> x0, waiting for transfers between devices: 20.6 us -> none
    all_gather x1 -> x0, blocking collectives: 14.8 us -> none  [local(): lax.all_gather(probes.astype(BF16), 'dp', axis=2, tiled=True).astype(F32)]
    pallas_call x0 -> x1, Pallas kernels: none -> 12.3 us  [settle(): pl.pallas_call(functools.partial(settle_kernel, scale, divisor), out_shap...]
  transfers between devices with their start and end apart: 2 -> 0, of which waited for: 2 -> 0; matrix products, arithmetic and copies ran while one was open for 0% -> 0% of each run, Pallas kernels for 0% -> 0%
where the time goes in v2:
time: 322 us
  Pallas kernels  318 us (99%)
  local copies, waits for them, and re-layouts  3.33 us (1%)
    pallas_call x1, Pallas kernels, relay(): pl.pallas_call(functools.partial(relay_kernel, sections, lag_step), out_s...  306 us
    pallas_call x1, Pallas kernels, settle(): pl.pallas_call(functools.partial(settle_kernel, scale, divisor), out_shap...  12.3 us

profile of v2, /device:TPU:0, one launch (start us, length us, event | category | flops | bytes accessed | tf_op | source)
XLA Modules:
  0.0 321.9 jit_solution(378969183047150007)
XLA Ops:
  0.6 1.3 copy.11
  1.9 0.0 copy-start.1
  1.9 305.5 %shard_map.68 = f32[2,4,1536]{2,1,0:T(4,128)} custom-call(bf16[8,16,3072]{2,1,0:T(8,128)(2,1)} %bitcast.20, bf16[8,16,1536]{2,1,0:T(8,128)(2,1)} %bitcast.21, f32[2,1,1536]{2,1,0:T(1,128)} %bitcast.22, f32[4,768]{1,0:T(4,128)} %bitcast.15, bf16[768,1536]{1,0:T(8,128)(2,1)} %bitcast.19), custom_call_target="tpu_custom_call" | custom-call | flops 12079595520 | bytes 9437184 | tf_op jit(solution)/shard_map/pallas_call | solution.py:581
  307.5 0.0 copy-done.1
  307.5 0.0 copy-start
  307.5 0.8 copy-done
  308.3 12.3 %shard_map.69 = (f32[4,768]{1,0:T(4,128)S(1)}, f32[4,768]{1,0:T(4,128)S(1)}) custom-call(f32[4,4,768]{2,1,0:T(4,128)S(1)} %bitcast.14, f32[4,768]{1,0:T(4,128)S(1)} %bitcast.16), custom_call_target="tpu_custom_call" | custom-call | tf_op jit(solution)/shard_map/pallas_call | solution.py:555
  320.6 0.6 copy.7
  321.2 0.6 copy.8
Async XLA Ops:
  1.9 305.5 %copy-start.1 = (f32[4,1,768]{2,0,1:T(4,128)S(1)}, f32[4,1,768]{2,0,1:T(4,128)}, u32[]{:S(2)}) copy-start(f32[4,1,768]{2,0,1:T(4,128)} %copy.11) | copy-start | bytes 36868
  307.5 0.8 copy-start

commit v3 on v2

--- a/solution.py
+++ b/solution.py
@@ -22,12 +22,379 @@
     return total
 
 
+def straight_gather(pos, last, core, weight_block_ref, weight_all, probe_block_ref, probe_all, right_send, right_recv, left_send, left_recv, probe_send, probe_recv, own_sem):
+    owners = lax.axis_size("dp")
+    me = lax.axis_index("dp")
+    depth = weight_block_ref.shape[0]
+    width = probe_block_ref.shape[1]
+    gather_probes = width < probe_all.shape[1]
+
+    barrier = pltpu.get_barrier_semaphore()
+    pl.semaphore_signal(barrier, inc=1, device_id={"mp": 1 - core}, device_id_type=MESH)
+
+    @pl.when(pos > 0)
+    def _():
+        pl.semaphore_signal(barrier, inc=1, device_id={"section": pos - 1}, device_id_type=MESH)
+
+    @pl.when(pos < last)
+    def _():
+        pl.semaphore_signal(barrier, inc=1, device_id={"section": pos + 1}, device_id_type=MESH)
+
+    def block_rows(b):
+        return pl.ds(pl.multiple_of(b * depth, depth), depth)
+
+    def greet(step, carry):
+        peer = lax.rem(me + step, owners)
+        pl.semaphore_signal(barrier, inc=1, device_id={"dp": peer}, device_id_type=MESH)
+        return carry
+
+    lax.fori_loop(1, owners, greet, 0)
+    own = pltpu.make_async_copy(weight_block_ref, weight_all.at[block_rows(me)], own_sem)
+    own.start()
+    peers = owners + (pos > 0).astype(jnp.int32) + (pos < last).astype(jnp.int32)
+    pl.semaphore_wait(barrier, peers)
+    own.wait()
+
+    def to_right(b):
+        return pltpu.make_async_remote_copy(
+            src_ref=weight_all.at[block_rows(b)],
+            dst_ref=weight_all.at[block_rows(b)],
+            send_sem=right_send.at[b],
+            recv_sem=right_recv.at[b],
+            device_id={"dp": me + 1},
+            device_id_type=MESH,
+        )
+
+    def to_left(b):
+        return pltpu.make_async_remote_copy(
+            src_ref=weight_all.at[block_rows(b)],
+            dst_ref=weight_all.at[block_rows(b)],
+            send_sem=left_send.at[b],
+            recv_sem=left_recv.at[b],
+            device_id={"dp": me - 1},
+            device_id_type=MESH,
+        )
+
+    @pl.when(me < owners - 1)
+    def _():
+        to_right(me).start()
+
+    @pl.when(me > 0)
+    def _():
+        to_left(me).start()
+
+    def probe_to(step):
+        mine = pl.ds(pl.multiple_of(me * width, width), width)
+        return pltpu.make_async_remote_copy(
+            src_ref=probe_all.at[:, mine],
+            dst_ref=probe_all.at[:, mine],
+            send_sem=probe_send.at[step],
+            recv_sem=probe_recv.at[step],
+            device_id={"dp": lax.rem(me + step, owners)},
+            device_id_type=MESH,
+        )
+
+    if gather_probes:
+        probe_all[:, pl.ds(pl.multiple_of(me * width, width), width)] = probe_block_ref[...]
+
+        def spread(step, carry):
+            probe_to(step).start()
+            return carry
+
+        lax.fori_loop(1, owners, spread, 0)
+    else:
+        probe_all[...] = probe_block_ref[...]
+
+
+    def relay_blocks(step, carry):
+        low, high = me - step, me + step
+
+        @pl.when(low >= 0)
+        def _():
+            to_right(low).wait_recv()
+
+            @pl.when(me < owners - 1)
+            def _():
+                to_right(low).start()
+
+        @pl.when(high < owners)
+        def _():
+            to_left(high).wait_recv()
+
+            @pl.when(me > 0)
+            def _():
+                to_left(high).start()
+
+        return carry
+
+    lax.fori_loop(1, owners, relay_blocks, 0)
+    if gather_probes:
+
+        def probes_in(step, carry):
+            probe_to(step).wait_recv()
+            return carry
+
+        lax.fori_loop(1, owners, probes_in, 0)
+
+
+    def drain():
+        def drain_blocks(b, carry):
+            @pl.when((me < owners - 1) & (b <= me))
+            def _():
+                to_right(b).wait_send()
+
+            @pl.when((me > 0) & (b >= me))
+            def _():
+                to_left(b).wait_send()
+
+            return carry
+
+        lax.fori_loop(0, owners, drain_blocks, 0)
+        if gather_probes:
+
+            def drain_probes(step, carry):
+                probe_to(step).wait_send()
+                return carry
+
+            lax.fori_loop(1, owners, drain_probes, 0)
+
+    return drain
+
+
+def crossed_gather(
+    inputs_arg, target_arg, gain_arg, probe_block_ref, weight_block_ref, weight_all, probe_all,
+    inputs_buf, target_buf, gain_buf, stage, sems, local_sems, one_sems,
+):
+    owners = lax.axis_size("dp")
+    plane, column, core = lax.axis_index("dp"), lax.axis_index("section"), lax.axis_index("mp")
+    depth = weight_block_ref.shape[0]
+    piece = depth // owners
+    width = probe_block_ref.shape[1]
+    place = plane * owners + column
+    out_send, out_recv, up_send, up_recv, x_send, x_recv, y_send, y_recv = [sems.at[i] for i in range(8)]
+    fx_send, fx_recv, fy_send, fy_recv, probe_send, probe_recv, gain_send = [sems.at[i] for i in range(8, 15)]
+
+    def flip(value, bits):
+        for bit in (1, 2):
+            if bits & bit:
+                value = value + bit - 2 * bit * (value // bit % 2)
+        return value
+
+    barrier = pltpu.get_barrier_semaphore()
+
+    def greet(step, carry):
+        peer = lax.rem(place + step, owners * owners)
+        target = {"dp": peer // owners, "section": lax.rem(peer, owners)}
+        pl.semaphore_signal(barrier, inc=1, device_id=target, device_id_type=MESH)
+        return carry
+
+    lax.fori_loop(1, owners * owners, greet, 0)
+    pl.semaphore_signal(barrier, inc=1, device_id={"mp": 1 - core}, device_id_type=MESH)
+    pl.semaphore_wait(barrier, owners * owners)
+
+    def remote(src, dst, send, recv, **target):
+        return pltpu.make_async_remote_copy(
+            src_ref=src, dst_ref=dst, send_sem=send, recv_sem=recv, device_id=target, device_id_type=MESH
+        )
+
+    def rows_of(k, t, start=0, count=piece):
+        return weight_all.at[pl.ds(pl.multiple_of(k * depth + t * piece + start, 16), count)]
+
+    def out(t):
+        src = weight_block_ref.at[pl.ds(pl.multiple_of(t * piece, 16), piece)]
+        return remote(src, stage.at[column], out_send.at[t], out_recv.at[column], section=t)
+
+    def out_in(s):
+        return remote(stage.at[s], stage.at[s], out_send.at[s], out_recv.at[s], section=s)
+
+    def up(r):
+        return remote(stage.at[r], rows_of(plane, column), up_send.at[r], up_recv.at[plane], dp=r)
+
+    def up_in(k):
+        return remote(stage.at[k], rows_of(k, column), up_send.at[k], up_recv.at[k], dp=k)
+
+    half = piece // 2
+    near_x, near_y, far = flip(column, 1), flip(column, 2), flip(column, 3)
+
+    def to_x(k, t):
+        return remote(rows_of(k, t), rows_of(k, t), x_send.at[k], x_recv.at[k], section=near_x)
+
+    def to_y(k, t):
+        return remote(rows_of(k, t), rows_of(k, t), y_send.at[k], y_recv.at[k], section=near_y)
+
+    def on_x(k, t):
+        rows = rows_of(k, t, half, half)
+        return remote(rows, rows, fx_send.at[k], fx_recv.at[k], section=near_x)
+
+    def on_y(k, t):
+        rows = rows_of(k, t, 0, half)
+        return remote(rows, rows, fy_send.at[k], fy_recv.at[k], section=near_y)
+
+    first_stage = pltpu.make_async_copy(
+        weight_block_ref.at[pl.ds(pl.multiple_of(column * piece, 16), piece)], stage.at[column], local_sems.at[0]
+    )
+    keep = pltpu.make_async_copy(stage.at[plane], rows_of(plane, column), local_sems.at[1])
+    for bits in (3, 1, 2):
+        out(flip(column, bits)).start()
+    first_stage.start()
+
+    def give_probe(t):
+        mine = probe_all.at[:, pl.ds(pl.multiple_of(plane * width, 128), width)]
+        return remote(probe_block_ref, mine, probe_send.at[t], probe_recv.at[plane], dp=column, section=t)
+
+    def take_probe(k):
+        mine = probe_all.at[:, pl.ds(pl.multiple_of(k * width, 128), width)]
+        return remote(probe_block_ref, mine, probe_send.at[k], probe_recv.at[k], dp=k, section=plane)
+
+    def give_gain(t):
+        return remote(gain_arg, gain_buf, gain_send.at[t], one_sems.at[0], section=t)
+
+    give_inputs = remote(inputs_arg, inputs_buf, one_sems.at[1], one_sems.at[2], dp=0)
+    give_target = remote(target_arg, target_buf, one_sems.at[3], one_sems.at[4], dp=owners - 1)
+    diagonal = plane == column
+    for t in range(owners):
+
+        @pl.when(~(diagonal & (column == t)))
+        def _():
+            give_probe(t).start()
+
+        @pl.when(diagonal & (column != t))
+        def _():
+            give_gain(t).start()
+
+    @pl.when(diagonal)
+    def _():
+        probe_all[:, pl.ds(pl.multiple_of(plane * width, 128), width)] = probe_block_ref[...]
+        gain_buf[...] = gain_arg[...]
+
+    @pl.when(diagonal & (plane != 0))
+    def _():
+        give_inputs.start()
+
+    @pl.when(diagonal & (plane == 0))
+    def _():
+        inputs_buf[...] = inputs_arg[...]
+
+    @pl.when(diagonal & (plane != owners - 1))
+    def _():
+        give_target.start()
+
+    @pl.when(diagonal & (plane == owners - 1))
+    def _():
+        target_buf[...] = target_arg[...]
+
+    def move_up(s):
+        @pl.when(s != plane)
+        def _():
+            up(s).start()
+
+        @pl.when(s == plane)
+        def _():
+            keep.start()
+
+    first_stage.wait()
+    move_up(column)
+    for bits in (1, 2, 3):
+        s = flip(column, bits)
+        out_in(s).wait_recv()
+        move_up(s)
+
+    def pass_on(k):
+        to_x(k, near_x).wait_recv()
+        on_y(k, near_x).start()
+        to_y(k, near_y).wait_recv()
+        on_x(k, near_y).start()
+
+    steps = [0]
+    for d in range(1, owners):
+        steps += [d, -d]
+
+    def when_valid(d, body):
+        k = plane + d
+
+        @pl.when((k >= 0) & (k < owners))
+        def _():
+            body(k)
+
+    def launch(k):
+        to_x(k, column).start()
+        to_y(k, column).start()
+
+    for index, d in enumerate(steps):
+        if d == 0:
+            keep.wait()
+            launch(plane)
+        else:
+
+            def arrive(k):
+                up_in(k).wait_recv()
+                launch(k)
+
+            when_valid(d, arrive)
+        if index > 0:
+            when_valid(steps[index - 1], pass_on)
+    when_valid(steps[-1], pass_on)
+    for k in range(owners):
+        on_x(k, far).wait_recv()
+        on_y(k, far).wait_recv()
+
+        @pl.when(~(diagonal & (plane == k)))
+        def _():
+            take_probe(k).wait_recv()
+
+    @pl.when(~diagonal)
+    def _():
+        give_gain(column).wait_recv()
+
+    @pl.when((plane == 0) & (column != 0))
+    def _():
+        give_inputs.wait_recv()
+
+    @pl.when((plane == owners - 1) & (column != owners - 1))
+    def _():
+        give_target.wait_recv()
+
+    def drain():
+        for k in range(owners):
+            to_x(k, column).wait_send()
+            to_y(k, column).wait_send()
+            on_x(k, near_y).wait_send()
+            on_y(k, near_x).wait_send()
+
+            @pl.when(column != k)
+            def _():
+                out(k).wait_send()
+
+            @pl.when(plane != k)
+            def _():
+                up(k).wait_send()
+
+            @pl.when(~(diagonal & (column == k)))
+            def _():
+                give_probe(k).wait_send()
+
+            @pl.when(diagonal & (column != k))
+            def _():
+                give_gain(k).wait_send()
+
+        @pl.when(diagonal & (plane != 0))
+        def _():
+            give_inputs.wait_send()
+
+        @pl.when(diagonal & (plane != owners - 1))
+        def _():
+            give_target.wait_send()
+
+    return drain
+
+
 def relay_kernel(
     sections,
     lag_step,
-    inputs_ref,
-    target_ref,
-    gain_ref,
+    crossed,
+    inputs_arg,
+    target_arg,
+    gain_arg,
     probe_block_ref,
     weight_block_ref,
     acc_ref,
@@ -59,96 +426,21 @@
     probe_send,
     probe_recv,
     own_sem,
+    *crossed_scratch,
 ):
-    pos = lax.axis_index("section")
+    pipe = "dp" if crossed else "section"
+    pos = lax.axis_index(pipe)
     core = lax.axis_index("mp")
     last = sections - 1
-    chunks, tokens, features = inputs_ref.shape
+    chunks, tokens, features = inputs_arg.shape
+    if crossed:
+        inputs_ref, target_ref, gain_ref = crossed_scratch[:3]
+    else:
+        inputs_ref, target_ref, gain_ref = inputs_arg, target_arg, gain_arg
     cols = features // 2
     dirs = probe_all.shape[0]
-    owners = lax.axis_size("dp")
-    me = lax.axis_index("dp")
-    depth = weight_block_ref.shape[0]
-    width = probe_block_ref.shape[1]
-    gather_probes = width < features
     tile = 512 if cols % 512 == 0 else 256 if cols % 256 == 0 else 128
     tiles = cols // tile
-
-    barrier = pltpu.get_barrier_semaphore()
-    pl.semaphore_signal(barrier, inc=1, device_id={"mp": 1 - core}, device_id_type=MESH)
-
-    @pl.when(pos > 0)
-    def _():
-        pl.semaphore_signal(barrier, inc=1, device_id={"section": pos - 1}, device_id_type=MESH)
-
-    @pl.when(pos < last)
-    def _():
-        pl.semaphore_signal(barrier, inc=1, device_id={"section": pos + 1}, device_id_type=MESH)
-
-    def block_rows(b):
-        return pl.ds(pl.multiple_of(b * depth, depth), depth)
-
-    def greet(step, carry):
-        peer = lax.rem(me + step, owners)
-        pl.semaphore_signal(barrier, inc=1, device_id={"dp": peer}, device_id_type=MESH)
-        return carry
-
-    lax.fori_loop(1, owners, greet, 0)
-    own = pltpu.make_async_copy(weight_block_ref, weight_all.at[block_rows(me)], own_sem)
-    own.start()
-    peers = owners + (pos > 0).astype(jnp.int32) + (pos < last).astype(jnp.int32)
-    pl.semaphore_wait(barrier, peers)
-    own.wait()
-
-    def to_right(b):
-        return pltpu.make_async_remote_copy(
-            src_ref=weight_all.at[block_rows(b)],
-            dst_ref=weight_all.at[block_rows(b)],
-            send_sem=right_send.at[b],
-            recv_sem=right_recv.at[b],
-            device_id={"dp": me + 1},
-            device_id_type=MESH,
-        )
-
-    def to_left(b):
-        return pltpu.make_async_remote_copy(
-            src_ref=weight_all.at[block_rows(b)],
-            dst_ref=weight_all.at[block_rows(b)],
-            send_sem=left_send.at[b],
-            recv_sem=left_recv.at[b],
-            device_id={"dp": me - 1},
-            device_id_type=MESH,
-        )
-
-    @pl.when(me < owners - 1)
-    def _():
-        to_right(me).start()
-
-    @pl.when(me > 0)
-    def _():
-        to_left(me).start()
-
-    def probe_to(step):
-        mine = pl.ds(pl.multiple_of(me * width, width), width)
-        return pltpu.make_async_remote_copy(
-            src_ref=probe_all.at[:, mine],
-            dst_ref=probe_all.at[:, mine],
-            send_sem=probe_send.at[step],
-            recv_sem=probe_recv.at[step],
-            device_id={"dp": lax.rem(me + step, owners)},
-            device_id_type=MESH,
-        )
-
-    if gather_probes:
-        probe_all[:, pl.ds(pl.multiple_of(me * width, width), width)] = probe_block_ref[...]
-
-        def spread(step, carry):
-            probe_to(step).start()
-            return carry
-
-        lax.fori_loop(1, owners, spread, 0)
-    else:
-        probe_all[...] = probe_block_ref[...]
 
     def hop(c):
         return pltpu.make_async_remote_copy(
@@ -156,7 +448,7 @@
             dst_ref=whole.at[c, core],
             send_sem=hop_send.at[c],
             recv_sem=hop_recv.at[c],
-            device_id={"section": pos + 1},
+            device_id={pipe: pos + 1},
             device_id_type=MESH,
         )
 
@@ -186,7 +478,7 @@
             dst_ref=cot_in.at[c],
             send_sem=back_send.at[c],
             recv_sem=back_recv.at[c],
-            device_id={"section": pos - 1},
+            device_id={pipe: pos - 1},
             device_id_type=MESH,
         )
 
@@ -201,35 +493,15 @@
 
     acc_ref[...] = jnp.zeros_like(acc_ref)
 
-    def relay_blocks(step, carry):
-        low, high = me - step, me + step
-
-        @pl.when(low >= 0)
-        def _():
-            to_right(low).wait_recv()
-
-            @pl.when(me < owners - 1)
-            def _():
-                to_right(low).start()
-
-        @pl.when(high < owners)
-        def _():
-            to_left(high).wait_recv()
-
-            @pl.when(me > 0)
-            def _():
-                to_left(high).start()
-
-        return carry
-
-    lax.fori_loop(1, owners, relay_blocks, 0)
-    if gather_probes:
-
-        def probes_in(step, carry):
-            probe_to(step).wait_recv()
-            return carry
-
-        lax.fori_loop(1, owners, probes_in, 0)
+    if crossed:
+        drain_gather = crossed_gather(
+            inputs_arg, target_arg, gain_arg, probe_block_ref, weight_block_ref, weight_all, probe_all, *crossed_scratch
+        )
+    else:
+        drain_gather = straight_gather(
+            pos, last, core, weight_block_ref, weight_all, probe_block_ref, probe_all,
+            right_send, right_recv, left_send, left_recv, probe_send, probe_recv, own_sem,
+        )
 
     def forward(c):
         @pl.when(pos == 0)
@@ -409,28 +681,10 @@
 
     lax.fori_loop(0, chunks, drain, 0)
 
-    def drain_blocks(b, carry):
-        @pl.when((me < owners - 1) & (b <= me))
-        def _():
-            to_right(b).wait_send()
-
-        @pl.when((me > 0) & (b >= me))
-        def _():
-            to_left(b).wait_send()
-
-        return carry
-
-    lax.fori_loop(0, owners, drain_blocks, 0)
-    if gather_probes:
-
-        def drain_probes(step, carry):
-            probe_to(step).wait_send()
-            return carry
-
-        lax.fori_loop(1, owners, drain_probes, 0)
-
-
-def settle_kernel(scale, divisor, parts_ref, probe_ref, hvp_ref, next_ref, got, tiles, sends, recvs, tile_sends, tile_recvs):
+    drain_gather()
+
+
+def settle_kernel(scale, divisor, crossed, parts_ref, probe_ref, hvp_ref, next_ref, got, tiles, sends, recvs, tile_sends, tile_recvs):
     owners, dirs, width = parts_ref.shape
     sections = lax.axis_size("section")
     dp, pos, core = lax.axis_index("dp"), lax.axis_index("section"), lax.axis_index("mp")
@@ -453,9 +707,20 @@
         pl.semaphore_signal(barrier, inc=1, device_id=target, device_id_type=MESH)
         return carry
 
-    lax.fori_loop(1, group, greet_owner, 0)
-    lax.fori_loop(0, owners * (sections - 1), greet_other, 0)
-    pl.semaphore_wait(barrier, group - 1 + owners * (sections - 1))
+    def greet_all(step, carry):
+        peer = lax.rem(place * 2 + core + step, 2 * everyone)
+        spot = peer // 2
+        target = {"dp": spot // sections, "section": lax.rem(spot, sections), "mp": lax.rem(peer, 2)}
+        pl.semaphore_signal(barrier, inc=1, device_id=target, device_id_type=MESH)
+        return carry
+
+    if crossed:
+        lax.fori_loop(1, 2 * everyone, greet_all, 0)
+        pl.semaphore_wait(barrier, 2 * everyone - 1)
+    else:
+        lax.fori_loop(1, group, greet_owner, 0)
+        lax.fori_loop(0, owners * (sections - 1), greet_other, 0)
+        pl.semaphore_wait(barrier, group - 1 + owners * (sections - 1))
 
     def give(step):
         peer = lax.rem(me + step, group)
@@ -472,13 +737,57 @@
         give(step).start()
         return carry
 
-    lax.fori_loop(1, group, start_give, 0)
-
     def take(step, total):
         give(step).wait_recv()
         return total + got[step]
 
-    curvature = lax.fori_loop(1, group, take, parts_ref[dp]) / divisor
+    def cross(slot):
+        spot = pos * 2 + core
+        return pltpu.make_async_remote_copy(
+            src_ref=parts_ref.at[slot // 2],
+            dst_ref=got.at[spot],
+            send_sem=sends.at[slot],
+            recv_sem=recvs.at[spot],
+            device_id={"dp": slot // 2, "section": dp, "mp": lax.rem(slot, 2)},
+            device_id_type=MESH,
+        )
+
+    def cross_in(slot):
+        return pltpu.make_async_remote_copy(
+            src_ref=got.at[slot],
+            dst_ref=got.at[slot],
+            send_sem=sends.at[slot],
+            recv_sem=recvs.at[slot],
+            device_id={"dp": pos, "section": slot // 2, "mp": lax.rem(slot, 2)},
+            device_id_type=MESH,
+        )
+
+    def away(slot):
+        return ~((dp == pos) & (slot == pos * 2 + core))
+
+    if crossed:
+        for slot in range(group):
+
+            @pl.when(away(slot))
+            def _():
+                cross(slot).start()
+
+        @pl.when(dp == pos)
+        def _():
+            got[pos * 2 + core] = parts_ref[dp]
+
+        total = jnp.zeros(probe_ref.shape, F32)
+        for slot in range(group):
+
+            @pl.when(away(slot))
+            def _():
+                cross_in(slot).wait_recv()
+
+            total = total + got[slot]
+        curvature = total / divisor
+    else:
+        lax.fori_loop(1, group, start_give, 0)
+        curvature = lax.fori_loop(1, group, take, parts_ref[dp]) / divisor
     hvp_ref[...] = curvature
     moved = probe_ref[...] + ETA * curvature
     row = lax.broadcasted_iota(jnp.int32, (16, 128), 0)
@@ -544,16 +853,24 @@
         tell(step).wait_send()
         return carry
 
-    lax.fori_loop(1, group, drain_give, 0)
+    if crossed:
+        for slot in range(group):
+
+            @pl.when(away(slot))
+            def _():
+                cross(slot).wait_send()
+
+    else:
+        lax.fori_loop(1, group, drain_give, 0)
     lax.fori_loop(1, everyone, drain_tell, 0)
 
 
-def settle(accumulated, own_probe, scale, divisor):
+def settle(accumulated, own_probe, scale, divisor, crossed):
     dirs, width = own_probe.shape
     owners, sections = lax.axis_size("dp"), lax.axis_size("section")
     vmem = pl.BlockSpec(memory_space=pltpu.VMEM)
     return pl.pallas_call(
-        functools.partial(settle_kernel, scale, divisor),
+        functools.partial(settle_kernel, scale, divisor, crossed),
         out_shape=[jax.ShapeDtypeStruct((dirs, width), F32)] * 2,
         in_specs=[vmem] * 2,
         out_specs=[vmem] * 2,
@@ -569,7 +886,7 @@
     )(accumulated.reshape(dirs, owners, width).transpose(1, 0, 2), own_probe)
 
 
-def relay(inputs, target, gain, probe, weight, sections, chunk_tokens, lag_step):
+def relay(inputs, target, gain, probe, weight, sections, chunk_tokens, lag_step, crossed):
     features = inputs.shape[-1]
     cols = features // 2
     dirs = probe.shape[0]
@@ -578,8 +895,19 @@
     vmem = pl.BlockSpec(memory_space=pltpu.VMEM)
     dma = pltpu.SemaphoreType.DMA((chunks,))
     ring = pltpu.SemaphoreType.DMA((lax.axis_size("dp"),))
+    extra = []
+    if crossed:
+        extra = [
+            pltpu.VMEM((chunks, chunk_tokens, features), BF16),
+            pltpu.VMEM((chunks, chunk_tokens, cols), BF16),
+            pltpu.VMEM((2, 1, cols), F32),
+            pltpu.VMEM((sections, weight.shape[0] // sections, cols), BF16),
+            pltpu.SemaphoreType.DMA((15, sections)),
+            pltpu.SemaphoreType.DMA((2,)),
+            pltpu.SemaphoreType.DMA((5,)),
+        ]
     acc = pl.pallas_call(
-        functools.partial(relay_kernel, sections, lag_step),
+        functools.partial(relay_kernel, sections, lag_step, crossed),
         out_shape=jax.ShapeDtypeStruct((2, dirs, cols), F32),
         in_specs=[vmem] * 4 + [pl.BlockSpec(memory_space=pl.ANY)],
         out_specs=vmem,
@@ -600,7 +928,8 @@
         ]
         + [dma] * 8
         + [ring] * 6
-        + [pltpu.SemaphoreType.DMA],
+        + [pltpu.SemaphoreType.DMA]
+        + extra,
         compiler_params=pltpu.CompilerParams(
             collective_id=0, has_side_effects=True, vmem_limit_bytes=56 * 1024 * 1024
         ),
@@ -621,11 +950,12 @@
     sections = lax.axis_size("section")
     batches, micro_batch_tokens, features = inputs.shape
     probe_block = probes[:, 0, :]
+    crossed = lax.axis_size("dp") == sections == 4 and probe_block.shape[1] % 128 == 0 and weights.shape[1] % 128 == 0
     if probe_block.shape[1] % 128:
         probe_block = lax.all_gather(probe_block, "dp", axis=1, tiled=True)
-    accumulated = relay(inputs, target, gains[0], probe_block, weights[0], sections, 16, 3)
+    accumulated = relay(inputs, target, gains[0], probe_block, weights[0], sections, 16, 3, crossed)
     divisor = batches * micro_batch_tokens * lax.axis_size("dp")
-    curvature, rotated = settle(accumulated, probes[:, 0, :], math.sqrt(sections * features), divisor)
+    curvature, rotated = settle(accumulated, probes[:, 0, :], math.sqrt(sections * features), divisor, crossed)
     return (curvature[:, None, :], rotated[:, None, :])
 
 

time: 322 us -> 300 us (0.932)
  Pallas kernels: 318 us -> 296 us
    pallas_call x2, Pallas kernels: 318 us -> 296 us  [the longest x1 283 us: relay(): pl.pallas_call(functools.partial(relay_kernel, sections, lag_step, crosse...]
where the time goes in v3:
time: 300 us
  Pallas kernels  296 us (99%)
  local copies, waits for them, and re-layouts  3.33 us (1%)
    pallas_call x1, Pallas kernels, relay(): pl.pallas_call(functools.partial(relay_kernel, sections, lag_step, crosse...  283 us
    pallas_call x1, Pallas kernels, settle(): pl.pallas_call(functools.partial(settle_kernel, scale, divisor, crossed),...  12.6 us

profile of v3, /device:TPU:0, one launch (start us, length us, event | category | flops | bytes accessed | tf_op | source)
XLA Modules:
  0.0 299.8 jit_solution(15904995286722911942)
XLA Ops:
  0.6 1.3 copy.11
  1.9 0.0 copy-start.1
  1.9 283.2 %shard_map.68 = f32[2,4,1536]{2,1,0:T(4,128)} custom-call(bf16[8,16,3072]{2,1,0:T(8,128)(2,1)} %bitcast.20, bf16[8,16,1536]{2,1,0:T(8,128)(2,1)} %bitcast.21, f32[2,1,1536]{2,1,0:T(1,128)} %bitcast.22, f32[4,768]{1,0:T(4,128)} %bitcast.15, bf16[768,1536]{1,0:T(8,128)(2,1)} %bitcast.19), custom_call_target="tpu_custom_call" | custom-call | flops 12079595520 | bytes 9437184 | tf_op jit(solution)/shard_map/pallas_call | solution.py:909
  285.1 0.0 copy-done.1
  285.1 0.0 copy-start
  285.1 0.8 copy-done
  285.9 12.6 %shard_map.69 = (f32[4,768]{1,0:T(4,128)S(1)}, f32[4,768]{1,0:T(4,128)S(1)}) custom-call(f32[4,4,768]{2,1,0:T(4,128)S(1)} %bitcast.14, f32[4,768]{1,0:T(4,128)S(1)} %bitcast.16), custom_call_target="tpu_custom_call" | custom-call | tf_op jit(solution)/shard_map/pallas_call | solution.py:872
  298.6 0.6 copy.7
  299.2 0.6 copy.8
Async XLA Ops:
  1.9 283.2 %copy-start.1 = (f32[4,1,768]{2,0,1:T(4,128)S(1)}, f32[4,1,768]{2,0,1:T(4,128)}, u32[]{:S(2)}) copy-start(f32[4,1,768]{2,0,1:T(4,128)} %copy.11) | copy-start | bytes 36868
  285.1 0.8 copy-start

commit v4 on v3

--- a/solution.py
+++ b/solution.py
@@ -283,21 +283,10 @@
     def _():
         target_buf[...] = target_arg[...]
 
-    def move_up(s):
-        @pl.when(s != plane)
-        def _():
-            up(s).start()
-
-        @pl.when(s == plane)
-        def _():
-            keep.start()
-
     first_stage.wait()
-    move_up(column)
     for bits in (1, 2, 3):
-        s = flip(column, bits)
-        out_in(s).wait_recv()
-        move_up(s)
+        out_in(flip(column, bits)).wait_recv()
+    keep.start()
 
     def pass_on(k):
         to_x(k, near_x).wait_recv()
@@ -320,7 +309,19 @@
         to_x(k, column).start()
         to_y(k, column).start()
 
+    def send_up(k):
+        up(k).start()
+
+    def sent_up(k):
+        up(k).wait_send()
+
     for index, d in enumerate(steps):
+        if d >= 0:
+            for sign in (1, -1):
+                if d > 0:
+                    when_valid(sign * d, sent_up)
+                if d + 1 < owners:
+                    when_valid(sign * (d + 1), send_up)
         if d == 0:
             keep.wait()
             launch(plane)
@@ -364,10 +365,6 @@
             @pl.when(column != k)
             def _():
                 out(k).wait_send()
-
-            @pl.when(plane != k)
-            def _():
-                up(k).wait_send()
 
             @pl.when(~(diagonal & (column == k)))
             def _():
@@ -544,8 +541,8 @@
                     mixed = (t * s + h * u[k]) * gain + n * probe_at(half, k, at)
                     operand[half, rows(k + 1), at] = mixed.astype(BF16)
 
-        def product(j, carry):
-            at = pl.ds(pl.multiple_of(j * tile, tile), tile)
+        for j in range(tiles):
+            at = pl.ds(j * tile, tile)
             a = jnp.dot(operand[0], weight_all[0:cols, at], preferred_element_type=F32)
             a = a + jnp.dot(operand[1], weight_all[cols:, at], preferred_element_type=F32)
             b = jnp.tanh(a[0:tokens])
@@ -556,9 +553,6 @@
                 bk = slope * a[k * tokens : (k + 1) * tokens]
                 act[c, rows(k), at] = bk
                 out[c, rows(k), at] = (whole[c, core, rows(k), at].astype(F32) + bk).astype(BF16)
-            return carry
-
-        lax.fori_loop(0, tiles, product, 0)
 
         @pl.when(pos < last)
         def _():
@@ -591,10 +585,10 @@
 
         def product(j, sums):
             half = j // tiles
-            at = pl.ds(pl.multiple_of((j % tiles) * tile, tile), tile)
+            at = pl.ds((j % tiles) * tile, tile)
             q_all = lax.dot_general(
                 gstack[...],
-                weight_all[pl.ds(pl.multiple_of(j * tile, tile), tile), :],
+                weight_all[pl.ds(j * tile, tile), :],
                 (((1,), (1,)), ((), ())),
                 preferred_element_type=F32,
             )
@@ -615,7 +609,9 @@
             return tuple(new)
 
         zero = jnp.zeros((tokens, 128), F32)
-        sums = lax.fori_loop(0, 2 * tiles, product, (zero,) * (dirs + 1))
+        sums = (zero,) * (dirs + 1)
+        for j in range(2 * tiles):
+            sums = product(j, sums)
 
         @pl.when(pos > 0)
         def _():

time: 300 us -> 271 us (0.903)
  Pallas kernels: 296 us -> 266 us
    pallas_call x1, Pallas kernels: 283 us -> 254 us  [relay(): pl.pallas_call(functools.partial(relay_kernel, sections, lag_step, crosse...]
where the time goes in v4:
time: 271 us; the launch traced here: 270 us
  Pallas kernels  266 us (98%)
  local copies, waits for them, and re-layouts  3.33 us (1%)
    pallas_call x1, Pallas kernels, relay(): pl.pallas_call(functools.partial(relay_kernel, sections, lag_step, crosse...  254 us
    pallas_call x1, Pallas kernels, settle(): pl.pallas_call(functools.partial(settle_kernel, scale, divisor, crossed),...  12.6 us

profile of v4, /device:TPU:0, one launch (start us, length us, event | category | flops | bytes accessed | tf_op | source)
XLA Modules:
  0.0 270.3 jit_solution(11540760301801253069)
XLA Ops:
  0.6 1.3 copy.11
  1.9 0.0 copy-start.1
  1.9 253.7 %shard_map.68 = f32[2,4,1536]{2,1,0:T(4,128)} custom-call(bf16[8,16,3072]{2,1,0:T(8,128)(2,1)} %bitcast.20, bf16[8,16,1536]{2,1,0:T(8,128)(2,1)} %bitcast.21, f32[2,1,1536]{2,1,0:T(1,128)} %bitcast.22, f32[4,768]{1,0:T(4,128)} %bitcast.15, bf16[768,1536]{1,0:T(8,128)(2,1)} %bitcast.19), custom_call_target="tpu_custom_call" | custom-call | flops 12079595520 | bytes 9437184 | tf_op jit(solution)/shard_map/pallas_call | solution.py:905
  255.7 0.0 copy-done.1
  255.7 0.0 copy-start
  255.7 0.8 copy-done
  256.5 12.6 %shard_map.69 = (f32[4,768]{1,0:T(4,128)S(1)}, f32[4,768]{1,0:T(4,128)S(1)}) custom-call(f32[4,4,768]{2,1,0:T(4,128)S(1)} %bitcast.14, f32[4,768]{1,0:T(4,128)S(1)} %bitcast.16), custom_call_target="tpu_custom_call" | custom-call | tf_op jit(solution)/shard_map/pallas_call | solution.py:868
  269.1 0.6 copy.7
  269.7 0.6 copy.8
Async XLA Ops:
  1.9 253.7 %copy-start.1 = (f32[4,1,768]{2,0,1:T(4,128)S(1)}, f32[4,1,768]{2,0,1:T(4,128)}, u32[]{:S(2)}) copy-start(f32[4,1,768]{2,0,1:T(4,128)} %copy.11) | copy-start | bytes 36868
  255.7 0.8 copy-start

commit v5 on v4

--- a/solution.py
+++ b/solution.py
@@ -439,22 +439,24 @@
     tile = 512 if cols % 512 == 0 else 256 if cols % 256 == 0 else 128
     tiles = cols // tile
 
-    def hop(c):
-        return pltpu.make_async_remote_copy(
-            src_ref=out.at[c],
-            dst_ref=whole.at[c, core],
-            send_sem=hop_send.at[c],
-            recv_sem=hop_recv.at[c],
+    def hop(c, j):
+        at = pl.ds(j * tile, tile)
+        return pltpu.make_async_remote_copy(
+            src_ref=out.at[c, :, at],
+            dst_ref=whole.at[c, core, :, at],
+            send_sem=hop_send.at[c, j],
+            recv_sem=hop_recv.at[c, j],
             device_id={pipe: pos + 1},
             device_id_type=MESH,
         )
 
-    def sibling(c):
-        return pltpu.make_async_remote_copy(
-            src_ref=whole.at[c, core],
-            dst_ref=whole.at[c, core],
-            send_sem=sib_send.at[c],
-            recv_sem=sib_recv.at[c],
+    def sibling(c, j):
+        at = pl.ds(j * tile, tile)
+        return pltpu.make_async_remote_copy(
+            src_ref=whole.at[c, core, :, at],
+            dst_ref=whole.at[c, core, :, at],
+            send_sem=sib_send.at[c, j],
+            recv_sem=sib_recv.at[c, j],
             device_id={"mp": 1 - core},
             device_id_type=MESH,
         )
@@ -509,10 +511,11 @@
 
         @pl.when(pos > 0)
         def _():
-            hop(c).wait_recv()
-            swap = sibling(c)
-            swap.start()
-            swap.wait_recv()
+            for j in range(tiles):
+                hop(c, j).wait_recv()
+                sibling(c, j).start()
+            for j in range(tiles):
+                sibling(c, j).wait_recv()
 
         square = jnp.zeros((tokens, 128), F32)
         cross = [jnp.zeros((tokens, 128), F32) for _ in range(dirs)]
@@ -554,9 +557,9 @@
                 act[c, rows(k), at] = bk
                 out[c, rows(k), at] = (whole[c, core, rows(k), at].astype(F32) + bk).astype(BF16)
 
-        @pl.when(pos < last)
-        def _():
-            hop(c).start()
+            @pl.when(pos < last)
+            def _(j=j):
+                hop(c, j).start()
 
     def backward(c):
         @pl.when(pos == last)
@@ -665,11 +668,13 @@
     def drain(c, carry):
         @pl.when(pos < last)
         def _():
-            hop(c).wait_send()
+            for j in range(tiles):
+                hop(c, j).wait_send()
 
         @pl.when(pos > 0)
         def _():
-            sibling(c).wait_send()
+            for j in range(tiles):
+                sibling(c, j).wait_send()
             part(c).wait_send()
             back(c).wait_send()
 
@@ -922,7 +927,8 @@
             pltpu.VMEM((2, height, cols), F32),
             pltpu.VMEM((chunks, dirs + 1, chunk_tokens, 128), F32),
         ]
-        + [dma] * 8
+        + [pltpu.SemaphoreType.DMA((chunks, cols // 128))] * 4
+        + [dma] * 4
         + [ring] * 6
         + [pltpu.SemaphoreType.DMA]
         + extra,

time: 271 us -> 273 us (level)
  Pallas kernels: 266 us -> 269 us
where the time goes in v5:
time: 273 us
  Pallas kernels  269 us (99%)
  local copies, waits for them, and re-layouts  3.33 us (1%)
    pallas_call x1, Pallas kernels, relay(): pl.pallas_call(functools.partial(relay_kernel, sections, lag_step, crosse...  256 us
    pallas_call x1, Pallas kernels, settle(): pl.pallas_call(functools.partial(settle_kernel, scale, divisor, crossed),...  12.7 us

profile of v5, /device:TPU:0, one launch (start us, length us, event | category | flops | bytes accessed | tf_op | source)
XLA Modules:
  0.0 272.6 jit_solution(15649858719927423590)
XLA Ops:
  0.6 1.3 copy.11
  1.9 0.0 copy-start.1
  1.9 255.9 %shard_map.68 = f32[2,4,1536]{2,1,0:T(4,128)} custom-call(bf16[8,16,3072]{2,1,0:T(8,128)(2,1)} %bitcast.20, bf16[8,16,1536]{2,1,0:T(8,128)(2,1)} %bitcast.21, f32[2,1,1536]{2,1,0:T(1,128)} %bitcast.22, f32[4,768]{1,0:T(4,128)} %bitcast.15, bf16[768,1536]{1,0:T(8,128)(2,1)} %bitcast.19), custom_call_target="tpu_custom_call" | custom-call | flops 12079595520 | bytes 9437184 | tf_op jit(solution)/shard_map/pallas_call | solution.py:910
  257.9 0.0 copy-done.1
  257.9 0.0 copy-start
  257.9 0.8 copy-done
  258.7 12.7 %shard_map.69 = (f32[4,768]{1,0:T(4,128)S(1)}, f32[4,768]{1,0:T(4,128)S(1)}) custom-call(f32[4,4,768]{2,1,0:T(4,128)S(1)} %bitcast.14, f32[4,768]{1,0:T(4,128)S(1)} %bitcast.16), custom_call_target="tpu_custom_call" | custom-call | tf_op jit(solution)/shard_map/pallas_call | solution.py:873
  271.3 0.6 copy.7
  272.0 0.6 copy.8
Async XLA Ops:
  1.9 255.9 %copy-start.1 = (f32[4,1,768]{2,0,1:T(4,128)S(1)}, f32[4,1,768]{2,0,1:T(4,128)}, u32[]{:S(2)}) copy-start(f32[4,1,768]{2,0,1:T(4,128)} %copy.11) | copy-start | bytes 36868
  257.9 0.8 copy-start
